TPU v7x, 256 devices: a whole 4x4x8 slice. The times are simulated.
256 devices in a mesh: grp: 8 (over y, core), dev: 32 (over x, z).
Axes of the slice: x: 4, y: 4, z: 8, core: 2. Of those that a mesh axis runs over, the one named last changes fastest.
Arguments:
- sample_field: float32 [2, 4096, 4096], P(None, 'grp', 'dev'), may hold values from -4 to 4
- probe_modes: float32 [2, 2, 256, 256], replicated, may hold values from -4 to 4
- amplitudes: float32 [1024, 256, 256], P(('grp', 'dev')), may hold values from 0.2 to 2.5
- rows_at: int32 [1024], P(('grp', 'dev')), may hold values from 0 to 3840, as said below
- cols_at: int32 [1024], P(('grp', 'dev')), may hold values from 0 to 3840, as said below
- live_counts: int32 [256], P(('grp', 'dev')), may hold values from 1 to 4, 512 in all
Outputs:
- new_sample: float32 [2, 4096, 4096], P(None, 'grp', 'dev')
- new_probe: float32 [2, 2, 256, 256], replicated
- probe_gradient: float32 [2, 2, 256, 256], replicated
Inputs may be any that keep to these rules, and one draw needn't show every extreme that they name: `rows_at`: a position held by the device at index g of grp starts at a row from g * 512 - 128 to g * 512 + 384, kept within the object. `cols_at`: a position held by the device at index d of dev starts at a column from d * 128 - 128 to d * 128, kept within the object. `live_counts`: slots at or past a device's count are unused.
All inputs are finite; a program needn't handle non-finite values.
Results may differ from a plain program's by a relative error of at most 0.006.
Values sent between devices are 32-bit elements; how exact they have to be, the bound alone decides.
A program may use at most 64 MiB of HBM per device.

v0:
```python
import math

import jax
import jax.numpy as jnp
from jax import lax
from jax.sharding import PartitionSpec as P

ITERS = 2


INTENSITY_FLOOR = 0.25
SAMPLE_DAMPING = 0.5
PROBE_DAMPING = 1.0


def with_halo(x, sides, width):
    for axis, dim in sides:
        devices, length = (lax.axis_size(axis), x.shape[dim])
        up = [(i, (i + 1) % devices) for i in range(devices - 1)]
        down = [(j, i) for i, j in up]
        last = lax.slice_in_dim(x, length - width, length, axis=dim)
        leading = lax.slice_in_dim(x, 0, width, axis=dim)
        before = lax.ppermute(last, axis, up)
        after = lax.ppermute(leading, axis, down)
        x = jnp.concatenate([before, x, after], axis=dim)
    return x


def shifted(x, axis, by):
    devices = lax.axis_size(axis)
    pairs = [(i, i + by) for i in range(devices) if 0 <= i + by < devices]
    return lax.ppermute(x, axis, pairs)


def dft_tables(pixels):
    indices = jnp.arange(pixels, dtype=jnp.int32)
    phases = indices[:, None] * indices[None, :] % pixels
    angles = phases.astype(jnp.float32) * (2.0 * math.pi / pixels)
    scaling = 1.0 / math.sqrt(pixels)
    return jnp.stack([jnp.cos(angles) * scaling, jnp.sin(angles) * scaling]).astype(jnp.bfloat16)


def combine(products, sign_factor):
    real_part = products[0][:, 0] + sign_factor * products[1][:, 1]
    imag_part = products[0][:, 1] - sign_factor * products[1][:, 0]
    return jnp.stack([real_part, imag_part], axis=1)


def transform(values, tables, sign_factor):
    first = jnp.einsum("tab,mcbk->tmcak", tables, values, preferred_element_type=jnp.float32)
    rows_done = combine(first, sign_factor).astype(jnp.bfloat16)
    second = jnp.einsum("mcaj,tjk->tmcak", rows_done, tables, preferred_element_type=jnp.float32)
    return combine(second, sign_factor)


def position_terms(patch_field, probe_modes, amplitude, tables):
    sample_re = patch_field[0]
    sample_im = patch_field[1]
    probe_re = probe_modes[:, 0]
    probe_im = probe_modes[:, 1]
    wave_re = probe_re * sample_re - probe_im * sample_im
    wave_im = probe_re * sample_im + probe_im * sample_re
    exit_wave = jnp.stack([wave_re, wave_im], axis=1).astype(jnp.bfloat16)
    spectrum = transform(exit_wave, tables, 1.0)
    intensity = jnp.sum(spectrum[:, 0] ** 2 + spectrum[:, 1] ** 2, axis=0)
    factor = amplitude / jnp.sqrt(jnp.maximum(intensity, INTENSITY_FLOOR)) - 1.0
    corrected = (spectrum * factor).astype(jnp.bfloat16)
    chi_field = transform(corrected, tables, -1.0)
    back_re = chi_field[:, 0]
    back_im = chi_field[:, 1]
    grad_re = jnp.sum(probe_re * back_re + probe_im * back_im, axis=0)
    grad_im = jnp.sum(probe_re * back_im - probe_im * back_re, axis=0)
    lighting = jnp.sum(probe_re**2 + probe_im**2, axis=0)
    sample_term = jnp.stack([grad_re, grad_im, lighting])
    probe_re_term = sample_re * back_re + sample_im * back_im
    probe_im_term = sample_re * back_im - sample_im * back_re
    probe_term = jnp.stack([probe_re_term, probe_im_term], axis=1)
    return (sample_term, probe_term, sample_re**2 + sample_im**2)


def local(sample_field, probe_modes, amplitudes, rows_at, cols_at, live_counts):
    patch_width = probe_modes.shape[2]
    margin = patch_width // 2
    band_rows = sample_field.shape[1]
    tile_cols = sample_field.shape[2]
    capacity = amplitudes.shape[0]
    total_slots = capacity * lax.axis_size("grp") * lax.axis_size("dev")
    tables = dft_tables(patch_width)
    row_anchor = lax.axis_index("grp") * band_rows - margin
    col_anchor = lax.axis_index("dev") * tile_cols - margin
    live_count = live_counts[0]
    probe_grad = jnp.zeros(probe_modes.shape, jnp.float32)
    for iteration in range(ITERS):
        extended = with_halo(sample_field, (("grp", 1), ("dev", 2)), margin)
        current_probe = probe_modes

        def visit_one(slot_index, state):
            totals, probe_sum, probe_weight = state
            row_start = rows_at[slot_index] - row_anchor
            col_start = cols_at[slot_index] - col_anchor
            anchor = (jnp.int32(0), row_start, col_start)
            patch_field = lax.dynamic_slice(extended, anchor, (2, patch_width, patch_width))
            sample_term, probe_term, weight_term = position_terms(
                patch_field, current_probe, amplitudes[slot_index], tables
            )
            previous = lax.dynamic_slice(totals, anchor, (3, patch_width, patch_width))
            totals = lax.dynamic_update_slice(totals, previous + sample_term, anchor)
            return (totals, probe_sum + probe_term, probe_weight + weight_term)

        initial = (
            jnp.zeros((3, band_rows + 2 * margin, tile_cols + 2 * margin), jnp.float32),
            jnp.zeros(probe_modes.shape, jnp.float32),
            jnp.zeros((patch_width, patch_width), jnp.float32),
        )

        def guarded(slot_index, state):
            return lax.cond(
                slot_index < live_count,
                lambda inner: visit_one(slot_index, inner),
                lambda inner: inner,
                state,
            )

        totals, probe_grad, probe_weight = lax.fori_loop(0, capacity, guarded, initial)
        from_next = shifted(totals[:, :, :margin], "dev", -1)
        from_prev = shifted(totals[:, :, margin + tile_cols :], "dev", 1)
        columns = totals[:, :, margin : margin + tile_cols] + from_next + from_prev
        from_below = shifted(columns[:, :margin], "grp", -1)
        from_above = shifted(columns[:, margin + band_rows :], "grp", 1)
        owned = columns[:, margin : margin + band_rows]
        owned = owned.at[:, band_rows - margin :].add(from_below)
        owned = owned.at[:, :margin].add(from_above)
        owned_grad = owned[:2]
        owned_light = owned[2]
        probe_grad, probe_weight = lax.psum((probe_grad, probe_weight), ("grp", "dev"))
        sample_field = sample_field + owned_grad / (owned_light + SAMPLE_DAMPING)
        probe_modes = current_probe + probe_grad / (probe_weight + PROBE_DAMPING)
    return (sample_field, probe_modes, probe_grad * (1.0 / math.sqrt(total_slots)))


def solution(mesh):
    return jax.shard_map(
        local,
        mesh=mesh,
        in_specs=(
            P(None, "grp", "dev"),
            P(),
            P(("grp", "dev"), None, None),
            P(("grp", "dev")),
            P(("grp", "dev")),
            P(("grp", "dev")),
        ),
        out_specs=(P(None, "grp", "dev"), P(), P()),
        check_vma=False,
    )
```

profile of v0, /device:TPU:1, one launch (start us, length us, event | category | flops | bytes accessed | tf_op | source)
XLA Modules:
  0.0 822.7 jit_solution(5733850099569760043)
XLA Ops:
  8.6 4.6 collective-permute-start
  15.1 4.3 collective-permute-done.1
  21.7 5.1 collective-permute-start.2
  28.3 11.0 %collective-permute-done.3 = f32[2,768,128]{1,2,0:T(8,128)} collective-permute-done((f32[2,768,128]{1,2,0:T(8,128)}, f32[2,768,128]{1,2,0:T(8,128)}, u32[]{:S(2)}, u32[]{:S(2)}) %collective-permute-start.3) | collective-permute-done | bytes 786464 | tf_op jit(solution)/shard_map/ppermute | solution.py:24
  41.0 3.0 pad_maximum_fusion
  44.1 2.0 broadcast.246.clone
  46.2 21.1 %while.38 = (s32[]{:T(128)}, f32[3,768,384]{1,2,0:T(8,128)}, f32[2,2,256,256]{2,3,1,0:T(8,128)S(1)}, f32[256,256]{0,1:T(8,128)S(1)}, s32[]{:T(128)}, /*index=5*/...) while((s32[]{:T(128)}, f32[3,768,384]{1,2,0:T(8,128)}, ...), condition=%wide.region_7.8_spmd, body=%wide.region_0.7_spmd.sunk | while | flops 1085014016 | bytes 57410032 | solution.py:124
  46.8 18.4 %conditional.4 = ((f32[3,768,384]{1,2,0:T(8,128)}, f32[2,2,256,256]{2,3,1,0:T(8,128)S(1)}, f32[256,256]{0,1:T(8,128)S(1)})) conditional(s32[]{:T(128)} %convert_element_type.61, (f32[3,768,384]{1,2,0:T(8,128)}, f32[2,2,256,256]{2,3,1,0:T(8,128)S(1)}, f32[256,256]{0,1:T(8,128)S(1)}) %tuple.132, (s32[]{:T(128)}, s32[4]{0:T(128)S(1)}, s32[]{:T(128)}, ...), branch_computations={%region_1.1_spmd, %region_2.6_spmd} | conditional | flops 1085014016 | bytes 57409756 | solution.py:117
  57.4 7.9 dynamic_update_slice.4
  67.3 5.2 copy.51
  75.7 5.8 collective-permute-start.5
  81.5 11.6 %collective-permute-done.4 = f32[3,768,128]{2,1,0:T(8,128)S(1)} collective-permute-done((f32[3,768,128]{2,1,0:T(8,128)S(1)}, f32[3,768,128]{2,1,0:T(8,128)S(1)}, u32[]{:S(2)}, u32[]{:S(2)}) %collective-permute-start.4) | collective-permute-done | bytes 1179680 | tf_op jit(solution)/shard_map/ppermute | solution.py:32
  96.8 19.8 %collective-permute-start.6 = (f32[3,128,128]{2,1,0:T(8,128)}, f32[3,128,128]{2,1,0:T(8,128)S(1)}, u32[]{:S(2)}, u32[]{:S(2)}) collective-permute-start(f32[3,128,128]{2,1,0:T(8,128)} %get-tuple-element.760), channel_id=1, source_target_pairs={{32,0},{64,32},{96,64},{128,96},{160,128},{192,160},{224,192},{33,... | collective-permute-start | bytes 589832 | tf_op jit(solution)/shard_map/ppermute | solution.py:32
  118.0 23.9 %collective-permute-start.7 = (f32[3,128,128]{2,1,0:T(8,128)S(1)}, f32[3,128,128]{2,1,0:T(8,128)S(1)}, u32[]{:S(2)}, u32[]{:S(2)}) collective-permute-start(f32[3,128,128]{2,1,0:T(8,128)S(1)} %get-tuple-element.759), channel_id=1, source_target_pairs={{0,32},{32,64},{64,96},{96,128},{128,160},{160,192},{192,224},{1,3... | collective-permute-start | bytes 589832 | tf_op jit(solution)/shard_map/ppermute | solution.py:32
  141.9 2.5 collective-permute-done.7
  144.6 4.5 collective-permute-start.8
  151.1 4.3 collective-permute-done.9
  157.7 25.9 %collective-permute-start.10 = (f32[2,768,128]{2,1,0:T(8,128)}, f32[2,768,128]{2,1,0:T(8,128)}, u32[]{:S(2)}, u32[]{:S(2)}) collective-permute-start(f32[2,768,128]{2,1,0:T(8,128)} %pad_maximum_fusion.3), channel_id=1, source_target_pairs={{0,1},{1,2},{2,3},{3,4},{4,5},{5,6},{6,7},{7,8},{8,9},{9,10},{10,1... | collective-permute-start | bytes 2359304 | tf_op jit(solution)/shard_map/ppermute | solution.py:23
  183.6 251.0 %all-reduce.7.cloned.1.call-done = (f32[2,2,256,256]{3,2,1,0:T(8,128)}, f32[256,256]{0,1:T(8,128)}) async-done(((f32[2,2,256,256]{3,2,1,0:T(8,128)}, f32[256,256]{0,1:T(8,128)}), (f32[2,2,256,256]{3,2,1,0:T(8,128)}, f32[256,256]{0,1:T(8,128)})) %all-reduce.7.cloned.1.call-update) | async-done | bytes 1310736 | tf_op jit(solution)/shard_map/psum | solution.py:135
  438.2 3.0 pad_maximum_fusion.1
  441.1 3.1 copy.57
  444.3 2.1 broadcast.246
  446.4 21.4 %while.39 = (s32[]{:T(128)}, f32[3,768,384]{1,2,0:T(8,128)}, f32[2,2,256,256]{2,3,1,0:T(8,128)S(1)}, f32[256,256]{0,1:T(8,128)S(1)}, s32[]{:T(128)}, /*index=5*/...) while((s32[]{:T(128)}, f32[3,768,384]{1,2,0:T(8,128)}, ...), condition=%wide.region_17.0_spmd, body=%wide.region_10.17_spmd.sunk | while | flops 1085014016 | bytes 57410032 | solution.py:124
  447.0 18.6 %conditional.5 = ((f32[3,768,384]{1,2,0:T(8,128)}, f32[2,2,256,256]{2,3,1,0:T(8,128)S(1)}, f32[256,256]{0,1:T(8,128)S(1)})) conditional(s32[]{:T(128)} %convert_element_type.62, (f32[3,768,384]{1,2,0:T(8,128)}, f32[2,2,256,256]{2,3,1,0:T(8,128)S(1)}, f32[256,256]{0,1:T(8,128)S(1)}) %tuple.135, (s32[]{:T(128)}, s32[4]{0:T(128)S(1)}, s32[]{:T(128)}, ...), branch_computations={%region_11.11_spmd, %region_12.16_spmd} | conditional | flops 1085014016 | bytes 57409756 | solution.py:117
  457.8 7.9 dynamic_update_slice.5
  467.7 5.3 copy.58
  473.0 3.2 fusion.74
  477.5 6.4 collective-permute-start.13
  485.3 315.2 %all-reduce.5.cloned.1.call-done = (f32[2,2,256,256]{3,2,1,0:T(8,128)}, f32[256,256]{0,1:T(8,128)}) async-done(((f32[2,2,256,256]{3,2,1,0:T(8,128)}, f32[256,256]{0,1:T(8,128)}), (f32[2,2,256,256]{3,2,1,0:T(8,128)}, f32[256,256]{0,1:T(8,128)})) %all-reduce.5.cloned.1.call-update) | async-done | bytes 1310736 | tf_op jit(solution)/shard_map/psum | solution.py:135
  803.5 4.0 collective-permute-start.14
  809.1 3.2 collective-permute-start.15
  812.4 2.6 collective-permute-done.15
  (130 shorter events, 51.6 us)
Async XLA Ops:
  7.2 19.6 %copy-start.6 = (f32[2,2,256,256]{3,2,1,0:T(8,128)S(1)}, f32[2,2,256,256]{3,2,1,0:T(8,128)}, u32[]{:S(2)}) copy-start(f32[2,2,256,256]{3,2,1,0:T(8,128)} %param.23) | copy-start | bytes 3145732
  7.2 427.4 %all-reduce.7.cloned.1.call-start = ((), (), s32[]{:S(2)}) async-start(), calls=%async_computation.1 | async-start | bytes 2621440 | tf_op jit(solution)/shard_map/psum | solution.py:135
  8.6 6.5 collective-permute-start
  13.2 6.3 collective-permute-start.1
  20.4 18.9 %collective-permute-start.3 = (f32[2,768,128]{1,2,0:T(8,128)}, f32[2,768,128]{1,2,0:T(8,128)}, u32[]{:S(2)}, u32[]{:S(2)}) collective-permute-start(f32[2,768,128]{1,2,0:T(8,128)} %pad_maximum_fusion.2), channel_id=1, source_target_pairs={{1,0},{2,1},{3,2},{4,3},{5,4},{6,5},{7,6},{8,7},{9,8},{10,9},{11,1... | collective-permute-start | bytes 2359304 | tf_op jit(solution)/shard_map/ppermute | solution.py:24
  21.7 19.4 %collective-permute-start.2 = (f32[2,768,128]{1,2,0:T(8,128)}, f32[2,768,128]{1,2,0:T(8,128)}, u32[]{:S(2)}, u32[]{:S(2)}) collective-permute-start(f32[2,768,128]{1,2,0:T(8,128)} %pad_maximum_fusion.2), channel_id=1, source_target_pairs={{0,1},{1,2},{2,3},{3,4},{4,5},{5,6},{6,7},{7,8},{8,9},{9,10},{10,1... | collective-permute-start | bytes 2359304 | tf_op jit(solution)/shard_map/ppermute | solution.py:23
  44.0 2.1 copy-start.12
  44.1 2.1 copy-start.13
  67.3 5.3 copy-start.1
  74.4 18.7 %collective-permute-start.4 = (f32[3,768,128]{2,1,0:T(8,128)S(1)}, f32[3,768,128]{2,1,0:T(8,128)S(1)}, u32[]{:S(2)}, u32[]{:S(2)}) collective-permute-start(f32[3,768,128]{2,1,0:T(8,128)S(1)} %get-tuple-element.755), channel_id=1, source_target_pairs={{1,0},{2,1},{3,2},{4,3},{5,4},{6,5},{7,6},{8,7},{9,8},{10,9},{11,1... | collective-permute-start | bytes 3538952 | tf_op jit(solution)/shard_map/ppermute | solution.py:32
  75.7 18.9 %collective-permute-start.5 = (f32[3,768,128]{2,1,0:T(8,128)S(1)}, f32[3,768,128]{2,1,0:T(8,128)S(1)}, u32[]{:S(2)}, u32[]{:S(2)}) collective-permute-start(f32[3,768,128]{2,1,0:T(8,128)S(1)} %get-tuple-element.756), channel_id=1, source_target_pairs={{0,1},{1,2},{2,3},{3,4},{4,5},{5,6},{6,7},{7,8},{8,9},{9,10},{10,1... | collective-permute-start | bytes 3538952 | tf_op jit(solution)/shard_map/ppermute | solution.py:32
  96.8 45.1 %collective-permute-start.6 = (f32[3,128,128]{2,1,0:T(8,128)}, f32[3,128,128]{2,1,0:T(8,128)S(1)}, u32[]{:S(2)}, u32[]{:S(2)}) collective-permute-start(f32[3,128,128]{2,1,0:T(8,128)} %get-tuple-element.760), channel_id=1, source_target_pairs={{32,0},{64,32},{96,64},{128,96},{160,128},{192,160},{224,192},{33,... | collective-permute-start | bytes 589832 | tf_op jit(solution)/shard_map/ppermute | solution.py:32
  117.8 26.7 %copy-start.8 = (f32[2,512,128]{2,1,0:T(8,128)S(1)}, f32[2,512,128]{2,1,0:T(8,128)}, u32[]{:S(2)}) copy-start(f32[2,512,128]{2,1,0:T(8,128)} %param.22) | copy-start | bytes 1572868
  117.8 682.6 %all-reduce.5.cloned.1.call-start = ((), (), s32[]{:S(2)}) async-start(), calls=%async_computation | async-start | bytes 2621440 | tf_op jit(solution)/shard_map/psum | solution.py:135
  118.0 26.5 %collective-permute-start.7 = (f32[3,128,128]{2,1,0:T(8,128)S(1)}, f32[3,128,128]{2,1,0:T(8,128)S(1)}, u32[]{:S(2)}, u32[]{:S(2)}) collective-permute-start(f32[3,128,128]{2,1,0:T(8,128)S(1)} %get-tuple-element.759), channel_id=1, source_target_pairs={{0,32},{32,64},{64,96},{96,128},{128,160},{160,192},{192,224},{1,3... | collective-permute-start | bytes 589832 | tf_op jit(solution)/shard_map/ppermute | solution.py:32
  144.5 291.2 %copy-start.7 = (f32[2,2,256,256]{3,2,1,0:T(8,128)S(1)}, f32[2,2,256,256]{3,2,1,0:T(8,128)}, u32[]{:S(2)}) copy-start(f32[2,2,256,256]{3,2,1,0:T(8,128)} %param.23) | copy-start | bytes 3145732
  144.6 292.9 %copy-start.2 = (f32[2,512,128]{2,1,0:T(8,128)}, f32[2,512,128]{2,1,0:T(8,128)S(1)}, u32[]{:S(2)}) copy-start(f32[2,512,128]{2,1,0:T(8,128)S(1)} %fusion.57) | copy-start | bytes 1572868
  144.6 6.5 collective-permute-start.8
  149.2 6.3 collective-permute-start.9
  155.4 279.2 %copy-start.10 = (f32[2,128,128]{2,1,0:T(8,128)}, f32[2,128,128]{2,1,0:T(8,128)S(1)}, u32[]{:S(2)}) copy-start(f32[2,128,128]{2,1,0:T(8,128)S(1)} %collective-permute-done.9) | copy-start | bytes 393220
  156.4 281.1 %collective-permute-start.11 = (f32[2,768,128]{2,1,0:T(8,128)}, f32[2,768,128]{2,1,0:T(8,128)}, u32[]{:S(2)}, u32[]{:S(2)}) collective-permute-start(f32[2,768,128]{2,1,0:T(8,128)} %pad_maximum_fusion.3), channel_id=1, source_target_pairs={{1,0},{2,1},{3,2},{4,3},{5,4},{6,5},{7,6},{8,7},{9,8},{10,9},{11,1... | collective-permute-start | bytes 2359304 | tf_op jit(solution)/shard_map/ppermute | solution.py:24
  157.7 279.8 %collective-permute-start.10 = (f32[2,768,128]{2,1,0:T(8,128)}, f32[2,768,128]{2,1,0:T(8,128)}, u32[]{:S(2)}, u32[]{:S(2)}) collective-permute-start(f32[2,768,128]{2,1,0:T(8,128)} %pad_maximum_fusion.3), channel_id=1, source_target_pairs={{0,1},{1,2},{2,3},{3,4},{4,5},{5,6},{6,7},{7,8},{8,9},{9,10},{10,1... | collective-permute-start | bytes 2359304 | tf_op jit(solution)/shard_map/ppermute | solution.py:23
  437.1 4.0 copy-start.4
  437.1 1.0 copy-start.11
  467.7 5.3 copy-start
  476.2 325.3 %collective-permute-start.12 = (f32[3,768,128]{2,1,0:T(8,128)}, f32[3,768,128]{2,1,0:T(8,128)S(1)}, u32[]{:S(2)}, u32[]{:S(2)}) collective-permute-start(f32[3,768,128]{2,1,0:T(8,128)} %get-tuple-element.753), channel_id=1, source_target_pairs={{1,0},{2,1},{3,2},{4,3},{5,4},{6,5},{7,6},{8,7},{9,8},{10,9},{11,1... | collective-permute-start | bytes 3538952 | tf_op jit(solution)/shard_map/ppermute | solution.py:32
  477.5 324.1 %collective-permute-start.13 = (f32[3,768,128]{2,1,0:T(8,128)}, f32[3,768,128]{2,1,0:T(8,128)}, u32[]{:S(2)}, u32[]{:S(2)}) collective-permute-start(f32[3,768,128]{2,1,0:T(8,128)} %get-tuple-element.754), channel_id=1, source_target_pairs={{0,1},{1,2},{2,3},{3,4},{4,5},{5,6},{6,7},{7,8},{8,9},{9,10},{10,1... | collective-permute-start | bytes 3538952 | tf_op jit(solution)/shard_map/ppermute | solution.py:32
  801.5 6.0 copy-start.5
  801.5 6.0 copy-start.9
  803.5 8.8 %collective-permute-start.14 = (f32[3,128,128]{2,1,0:T(8,128)S(1)}, f32[3,128,128]{2,1,0:T(8,128)S(1)}, u32[]{:S(2)}, u32[]{:S(2)}) collective-permute-start(f32[3,128,128]{2,1,0:T(8,128)S(1)} %get-tuple-element.758), channel_id=1, source_target_pairs={{32,0},{64,32},{96,64},{128,96},{160,128},{192,160},{224,192},{33,... | collective-permute-start | bytes 589832 | tf_op jit(solution)/shard_map/ppermute | solution.py:32
  809.1 5.9 copy-start.3
  809.1 5.8 collective-permute-start.15
Sparse Core Ops, SparseCore 0:
  118.0 316.5 all-reduce.6
  485.4 314.9 all-reduce.4
where the time goes:
time: 827 us; the launch traced here: 823 us
  waiting for transfers between devices  606 us (73%)
  starting transfers between devices  112 us (14%)
  local copies, waits for them, and re-layouts  48.7 us (6%)
  other arithmetic  29.2 us (4%)
  between operations  14.5 us (2%)
  loops' own time  8.4 us (1%)
    psum x2, waiting for transfers between devices, local(): lax.psum((probe_grad, probe_weight), ('grp', 'dev'))  566 us
    ppermute x8, starting transfers between devices, shifted(): return lax.ppermute(x, axis, pairs)  65.6 us
    ppermute x4, starting transfers between devices, with_halo(): before = lax.ppermute(last, axis, up)  40.1 us
    ppermute x4, waiting for transfers between devices, with_halo(): after = lax.ppermute(leading, axis, down)  19.7 us
    ppermute x8, waiting for transfers between devices, shifted(): return lax.ppermute(x, axis, pairs)  18.2 us
    while x7, local copies, waits for them, and re-layouts, local(): lax.fori_loop(0, capacity, guarded, initial)  16.8 us
  transfers between devices with their start and end apart: 18, of which 10 were waited for; matrix products, arithmetic and copies ran while one was open for 1% of the time, Pallas kernels for 0%

commit v1 on v0

v1 whole, which is shorter than its diff:
```python
import functools
import math

import jax
import jax.numpy as jnp
import ml_dtypes
import numpy as np
from jax import lax
from jax.experimental import pallas as pl
from jax.experimental.pallas import tpu as pltpu
from jax.sharding import PartitionSpec as P

INTENSITY_FLOOR = 0.25
SAMPLE_DAMPING = 0.5
PROBE_DAMPING = 1.0
MESH = pl.DeviceIdType.MESH
LANES = 128
N = 256
BAND = 512
EXT = BAND + 2 * LANES
FAR = 512
STEP = 16
COPIES = 112
UP, MIDDLE, DOWN = (0, 128), (128, 384), (384, 512)


def tables():
    k = np.arange(N)
    angles = (np.outer(k, k) % N).astype(np.float32) * np.float32(2.0 * math.pi / N)
    c = (np.cos(angles) / np.float32(16.0)).astype(ml_dtypes.bfloat16)
    s = (np.sin(angles) / np.float32(16.0)).astype(ml_dtypes.bfloat16)
    a = np.block([[c, s], [-s, c]])
    return a, np.ascontiguousarray(a.T)


def kernel(
    shape, sample, probe, amps, table_a, table_b, rows_at, cols_at, live,
    new_sample, new_probe, probe_gradient,
    field0, field1, probe0, probe1, amp, ta, tb, patch, wave, mid, spec, placed,
    up0, up1, dn0, dn1, own0, own1, fu0, fu1, fd0, fd1, fl0, fl1, fr0, fr1,
    part0, part1, rc0, rc1, hs0, hs1, rx0, rx1, hx0, hx1, ry0, ry1, zb0, zb1, rz0, rz1, zg0, zg1, full0, full1,
    load_sem, send_sem, recv_sem,
):
    nx, ny, nz = shape
    blocks = 2 * nx * ny
    depth = N // blocks
    zn = -(-10 // nz)
    field, prb = (field0, field1), (probe0, probe1)
    halo_up, halo_dn, own = (up0, up1), (dn0, dn1), (own0, own1)
    from_up, from_dn, from_left, from_right = (fu0, fu1), (fd0, fd1), (fl0, fl1), (fr0, fr1)
    part, rc, hs, rx, hx, ry = (part0, part1), (rc0, rc1), (hs0, hs1), (rx0, rx1), (hx0, hx1), (ry0, ry1)
    zb, rz, zg, full = (zb0, zb1), (rz0, rz1), (zg0, zg1), (full0, full1)

    g, d = lax.axis_index("grp"), lax.axis_index("dev")
    ng, nd = 2 * ny, nx * nz
    y, core = g // 2, g % 2
    x, z = d // nz, d % nz
    above = {"grp": (g + ng - 1) % ng, "dev": d}
    below = {"grp": (g + 1) % ng, "dev": d}
    left = {"grp": g, "dev": (d + nd - 1) % nd}
    right = {"grp": g, "dev": (d + 1) % nd}
    partner = {"grp": y * 2 + 1 - core, "dev": d}

    def along_x(k):
        xx = (x + k) % nx
        return xx, {"grp": g, "dev": xx * nz + z}

    def along_y(k):
        yy = (y + k) % ny
        return yy, {"grp": yy * 2 + core, "dev": d}

    def along_z(k):
        zz = (z + k) % nz
        return zz, {"grp": g, "dev": x * nz + zz}

    copies = []

    def send(src, dst, to):
        n = len(copies)
        copy = pltpu.make_async_remote_copy(
            src_ref=src, dst_ref=dst, send_sem=send_sem.at[n], recv_sem=recv_sem.at[n],
            device_id=to, device_id_type=MESH,
        )
        copy.start()
        copies.append(copy)
        return copy

    loads = [
        pltpu.make_async_copy(src, dst, load_sem.at[n])
        for n, (src, dst) in enumerate(
            (
                (sample, field0.at[1, :, LANES : LANES + BAND, :]),
                (probe, probe0),
                (table_a, ta),
                (table_b, tb),
                (amps, amp),
            )
        )
    ]
    for load in loads:
        load.start()

    barrier = pltpu.get_barrier_semaphore()
    peers = [above, below, left, right, partner]
    peers += [along_x(k)[1] for k in range(1, nx)]
    peers += [along_y(k)[1] for k in range(1, ny)]
    peers += [along_z(k)[1] for k in range(1, nz)]
    for peer in peers:
        pl.semaphore_signal(barrier, inc=1, device_id=peer, device_id_type=MESH)
    pl.semaphore_wait(barrier, len(peers))

    row_anchor = g * BAND - LANES
    col_anchor = d * LANES - LANES
    slots = 4
    starts = [jnp.clip(rows_at[p] - row_anchor, 0, FAR) for p in range(slots)]

    def send_columns(f, source, lo, hi):
        src = source(lo, hi)
        return (
            send(src, f.at[0, :, LANES + lo : LANES + hi, :], right),
            send(src, f.at[2, :, LANES + lo : LANES + hi, :], left),
        )

    def forward_up(f, t, src=None):
        src = f.at[t, :, LANES : 2 * LANES, :] if src is None else src
        return send(src, f.at[t, :, LANES + BAND : EXT, :], above)

    def forward_down(f, t, src=None):
        src = f.at[t, :, BAND : LANES + BAND, :] if src is None else src
        return send(src, f.at[t, :, 0:LANES, :], below)

    def spread(f, sent_up, sent_down, sent_middle, forwards):
        for copy in sent_up:
            copy.wait_recv()
        forwards += [forward_up(f, 0), forward_up(f, 2)]
        for copy in sent_down:
            copy.wait_recv()
        forwards += [forward_down(f, 0), forward_down(f, 2)]
        return list(sent_middle) + forwards

    def argument(lo, hi):
        return sample.at[:, lo:hi, :]

    sent_up = send_columns(field0, argument, *UP)
    sent_down = send_columns(field0, argument, *DOWN)
    forwards = [forward_up(field0, 1, argument(*UP)), forward_down(field0, 1, argument(*DOWN))]
    sent_middle = send_columns(field0, argument, *MIDDLE)

    def clear(i, _):
        zero = jnp.zeros((STEP, LANES), jnp.float32)
        rr = pl.multiple_of(i * STEP, STEP)
        for p in range(slots):
            for t in range(3):
                for ch in range(3):
                    placed[p, t, ch, pl.ds(rr, STEP), :] = zero
                    placed[p, t, ch, pl.ds(FAR + N + rr, STEP), :] = zero
        return 0

    lax.fori_loop(0, FAR // STEP, clear, 0)
    for it in range(2):
        part[it][...] = jnp.zeros(part[it].shape, jnp.float32)
        zb[it][...] = jnp.zeros(zb[it].shape, jnp.float32)

    waiting = spread(field0, sent_up, sent_down, sent_middle, forwards)
    for copy in waiting:
        copy.wait_recv()
    for load in loads:
        load.wait()

    def part_at(i8):
        if depth == 8:
            return i8, pl.ds(0, 8)
        per = depth // 8
        return i8 // per, pl.ds(pl.multiple_of(i8 % per * 8, 8), 8)

    def add_part(it, k, i, value):
        for e in range(STEP // 8):
            b, rows = part_at(i * (STEP // 8) + e)
            part[it][b, k, rows, :] += value[e * 8 : e * 8 + 8, :]

    def position(it, p):
        f, pr = field[it], prb[it]
        r0 = jnp.clip(rows_at[p] - row_anchor, 0, FAR)
        s = jnp.clip(cols_at[p] - col_anchor, 0, LANES)
        back = (LANES - s) % LANES
        ahead = s % LANES
        alive = jnp.full((STEP, LANES), p, jnp.int32) < jnp.full((STEP, LANES), live[0], jnp.int32)
        lane = lax.broadcasted_iota(jnp.int32, (STEP, LANES), 1)
        early = lane < LANES - s
        late = lane >= s

        def gather(i, _):
            rr = pl.multiple_of(i * STEP, STEP)
            rows = pl.ds(rr, STEP)
            halves = []
            for ch in range(2):
                a, b, c = (pltpu.roll(f[t, ch, pl.ds(r0 + rr, STEP), :], back, 1) for t in range(3))
                halves.append((jnp.where(early, a, b), jnp.where(early, b, c)))
            for j in range(2):
                o_re, o_im = halves[0][j], halves[1][j]
                patch[0, j, rows, :] = o_re
                patch[1, j, rows, :] = o_im
                add_part(it, 8 + j, i, jnp.where(alive, o_re * o_re + o_im * o_im, 0.0))
                for m in range(2):
                    cols = slice(m * N + j * LANES, m * N + (j + 1) * LANES)
                    p_re = pr[2 * m, rows, j * LANES : (j + 1) * LANES]
                    p_im = pr[2 * m + 1, rows, j * LANES : (j + 1) * LANES]
                    wave[rows, cols] = (p_re * o_re - p_im * o_im).astype(jnp.bfloat16)
                    wave[pl.ds(N + rr, STEP), cols] = (p_re * o_im + p_im * o_re).astype(jnp.bfloat16)
            return 0

        def columns_first(table):
            for m in range(2):
                for c in range(2):
                    mid[m * N : (m + 1) * N, c * N : (c + 1) * N] = jnp.dot(
                        table[c * N : (c + 1) * N, :],
                        wave[:, m * N : (m + 1) * N],
                        preferred_element_type=jnp.float32,
                    ).astype(jnp.bfloat16)

        def rows_next(table):
            for m in range(2):
                spec[m * N : (m + 1) * N, :] = jnp.dot(
                    mid[m * N : (m + 1) * N, :], table[...], preferred_element_type=jnp.float32
                )

        def correct(i, _):
            rr = pl.multiple_of(i * STEP, STEP)
            for j in range(2):
                values = [
                    [
                        spec[pl.ds(m * N + rr, STEP), c * N + j * LANES : c * N + (j + 1) * LANES]
                        for c in range(2)
                    ]
                    for m in range(2)
                ]
                intensity = (values[0][0] ** 2 + values[0][1] ** 2) + (
                    values[1][0] ** 2 + values[1][1] ** 2
                )
                measured = amp[p, pl.ds(rr, STEP), j * LANES : (j + 1) * LANES]
                factor = measured * lax.rsqrt(jnp.maximum(intensity, INTENSITY_FLOOR)) - 1.0
                for m in range(2):
                    for c in range(2):
                        wave[
                            pl.ds(c * N + rr, STEP), m * N + j * LANES : m * N + (j + 1) * LANES
                        ] = (values[m][c] * factor).astype(jnp.bfloat16)
            return 0

        def scatter(i, _):
            rr = pl.multiple_of(i * STEP, STEP)
            rows = pl.ds(rr, STEP)
            terms = []
            for j in range(2):
                o_re, o_im = patch[0, j, rows, :], patch[1, j, rows, :]
                g_re = g_im = light = jnp.zeros((STEP, LANES), jnp.float32)
                for m in range(2):
                    p_re = pr[2 * m, rows, j * LANES : (j + 1) * LANES]
                    p_im = pr[2 * m + 1, rows, j * LANES : (j + 1) * LANES]
                    b_re = spec[pl.ds(m * N + rr, STEP), j * LANES : (j + 1) * LANES]
                    b_im = spec[pl.ds(m * N + rr, STEP), N + j * LANES : N + (j + 1) * LANES]
                    g_re += p_re * b_re + p_im * b_im
                    g_im += p_re * b_im - p_im * b_re
                    light += p_re * p_re + p_im * p_im
                    h_re = o_re * b_re + o_im * b_im
                    h_im = o_re * b_im - o_im * b_re
                    add_part(it, 4 * m + j, i, jnp.where(alive, h_re, 0.0))
                    add_part(it, 4 * m + 2 + j, i, jnp.where(alive, h_im, 0.0))
                terms.append([jnp.where(alive, v, 0.0) for v in (g_re, g_im, light)])
            at = pl.ds(FAR + rr, STEP)
            for ch in range(3):
                a = pltpu.roll(terms[0][ch], ahead, 1)
                b = pltpu.roll(terms[1][ch], ahead, 1)
                placed[p, 0, ch, at, :] = jnp.where(late, a, 0.0)
                placed[p, 1, ch, at, :] = jnp.where(late, b, a)
                placed[p, 2, ch, at, :] = jnp.where(late, 0.0, b)
            return 0

        lax.fori_loop(0, N // STEP, gather, 0)
        columns_first(ta)
        rows_next(tb)
        lax.fori_loop(0, N // STEP, correct, 0)
        columns_first(tb)
        rows_next(ta)
        lax.fori_loop(0, N // STEP, scatter, 0)

    def total(dst, first, lo, hi):
        def body(i, _):
            rr = pl.multiple_of(lo + i * STEP, STEP)
            for t in range(3):
                for ch in range(3):
                    values = [
                        placed[p, t, ch, pl.ds(FAR + first + rr - starts[p], STEP), :] for p in range(slots)
                    ]
                    dst[t, ch, pl.ds(rr, STEP), :] = (values[0] + values[1]) + (values[2] + values[3])
            return 0

        lax.fori_loop(0, (hi - lo) // STEP, body, 0)

    def update(it, lo, hi):
        def body(i, _):
            rr = pl.multiple_of(lo + i * STEP, STEP)
            rows = pl.ds(rr, STEP)
            sums = [
                own[it][1, ch, rows, :] + (from_left[it][ch, rows, :] + from_right[it][ch, rows, :])
                for ch in range(3)
            ]
            scale = 1.0 / (sums[2] + SAMPLE_DAMPING)
            for ch in range(2):
                value = field[it][1, ch, pl.ds(LANES + rr, STEP), :] + sums[ch] * scale
                if it == 0:
                    field1[1, ch, pl.ds(LANES + rr, STEP), :] = value
                else:
                    new_sample[ch, rows, :] = value
            return 0

        lax.fori_loop(0, (hi - lo) // STEP, body, 0)

    def finish_probe(it):
        def body(i8, _):
            b, rows = part_at(i8)
            at = pl.ds(pl.multiple_of(i8 * 8, 8), 8)
            for j in range(2):
                cols = slice(j * LANES, (j + 1) * LANES)
                scale = 1.0 / (full[it][b, 8 + j, rows, :] + PROBE_DAMPING)
                for q in range(4):
                    grad = full[it][b, 2 * q + j, rows, :]
                    value = prb[it][q, at, cols] + grad * scale
                    if it == 0:
                        probe1[q, at, cols] = value
                    else:
                        new_probe[q, at, cols] = value
                        probe_gradient[q, at, cols] = grad * (1.0 / math.sqrt(slots * ng * nd))
            return 0

        lax.fori_loop(0, N // 8, body, 0)

    for it in range(2):
        lax.fori_loop(0, slots, lambda p, _: (position(it, p), 0)[1], 0)

        half = blocks // 2
        swap = send(part[it].at[pl.ds((1 - core) * half, half)], rc[it], partner)

        total(halo_up[it], 0, 0, LANES)
        rows_up = send(halo_up[it], from_dn[it], above)
        total(halo_dn[it], LANES + BAND, 0, LANES)
        rows_down = send(halo_dn[it], from_up[it], below)

        swap.wait_recv()

        def sum_core(i, _):
            hs[it][i] = part[it][core * half + i] + rc[it][i]
            return 0

        lax.fori_loop(0, half, sum_core, 0)
        to_x = []
        for k in range(1, nx):
            xx, peer = along_x(k)
            to_x.append(send(hs[it].at[pl.ds(xx * ny, ny)], rx[it].at[k - 1], peer))

        def send_sides(lo, hi):
            return (
                send(own[it].at[0, :, lo:hi, :], from_right[it].at[:, lo:hi, :], left),
                send(own[it].at[2, :, lo:hi, :], from_left[it].at[:, lo:hi, :], right),
            )

        total(own[it], LANES, *MIDDLE)
        side_middle = send_sides(*MIDDLE)
        total(own[it], LANES, *UP)
        total(own[it], LANES, *DOWN)

        def add_rows(src, lo):
            def body(i, _):
                rr = pl.multiple_of(i * STEP, STEP)
                for t in range(3):
                    for ch in range(3):
                        own[it][t, ch, pl.ds(lo + rr, STEP), :] += src[t, ch, pl.ds(rr, STEP), :]
                return 0

            lax.fori_loop(0, LANES // STEP, body, 0)

        rows_down.wait_recv()
        add_rows(from_up[it], UP[0])
        side_up = send_sides(*UP)
        rows_up.wait_recv()
        add_rows(from_dn[it], DOWN[0])
        side_down = send_sides(*DOWN)

        for copy in to_x:
            copy.wait_recv()
        for i in range(ny):
            value = hs[it][x * ny + i]
            for k in range(nx - 1):
                value += rx[it][k, i]
            hx[it][i] = value
        to_y = []
        for k in range(1, ny):
            yy, peer = along_y(k)
            to_y.append(send(hx[it].at[yy], ry[it].at[k - 1], peer))

        for copy in side_middle:
            copy.wait_recv()
        update(it, *MIDDLE)

        for copy in to_y:
            copy.wait_recv()
        value = hx[it][y]
        for k in range(ny - 1):
            value += ry[it][k]
        zb[it][0:10] = value
        to_z = []
        for k in range(1, nz):
            zz, peer = along_z(k)
            to_z.append(send(zb[it].at[pl.ds(zz * zn, zn)], rz[it].at[k - 1], peer))

        for copy in side_up:
            copy.wait_recv()
        update(it, *UP)
        if it == 0:

            def updated(lo, hi):
                return field1.at[1, :, LANES + lo : LANES + hi, :]

            sent_up = send_columns(field1, updated, *UP)
            forwards = [forward_up(field1, 1)]
        for copy in side_down:
            copy.wait_recv()
        update(it, *DOWN)
        if it == 0:
            sent_down = send_columns(field1, updated, *DOWN)
            forwards.append(forward_down(field1, 1))
            sent_middle = send_columns(field1, updated, *MIDDLE)

        for copy in to_z:
            copy.wait_recv()
        value = zb[it][pl.ds(z * zn, zn)]
        for k in range(nz - 1):
            value += rz[it][k]
        zg[it][pl.ds(z * zn, zn)] = value
        mine = zg[it].at[pl.ds(z * zn, zn)]
        back_z = [send(mine, mine, along_z(k)[1]) for k in range(1, nz)]
        for copy in back_z:
            copy.wait_recv()
        at = (core * nx + x) * ny + y
        full[it][at] = zg[it][0:10]
        mine = full[it].at[at]
        back_y = [send(mine, mine, along_y(k)[1]) for k in range(1, ny)]
        for copy in back_y:
            copy.wait_recv()
        mine = full[it].at[pl.ds((core * nx + x) * ny, ny)]
        back_x = [send(mine, mine, along_x(k)[1]) for k in range(1, nx)]
        if it == 0:
            waiting = spread(field1, sent_up, sent_down, sent_middle, forwards)
        for copy in back_x:
            copy.wait_recv()
        mine = full[it].at[pl.ds(core * half, half)]
        back_core = send(mine, mine, partner)
        back_core.wait_recv()
        finish_probe(it)
        if it == 0:
            for copy in waiting:
                copy.wait_recv()

    for copy in copies:
        copy.wait_send()


def solution(mesh):
    ng, nd = mesh.shape["grp"], mesh.shape["dev"]
    ny = ng // 2
    nx = 4 if nd == 32 else 2
    nz = nd // nx
    blocks = 2 * nx * ny
    depth = N // blocks
    zn = -(-10 // nz)
    table_a, table_b = tables()

    def two(shape, dtype=jnp.float32):
        return [pltpu.VMEM(shape, dtype)] * 2

    def local(sample, probe, amps, rows_at, cols_at, live):
        hbm = pl.BlockSpec(memory_space=pl.ANY)
        vmem = pl.BlockSpec(memory_space=pltpu.VMEM)
        smem = pl.BlockSpec(memory_space=pltpu.SMEM)
        new_sample, new_probe, probe_gradient = pl.pallas_call(
            functools.partial(kernel, (nx, ny, nz)),
            out_shape=[
                jax.ShapeDtypeStruct((2, BAND, LANES), jnp.float32),
                jax.ShapeDtypeStruct((4, N, N), jnp.float32),
                jax.ShapeDtypeStruct((4, N, N), jnp.float32),
            ],
            in_specs=[hbm] * 5 + [smem] * 3,
            out_specs=[vmem] * 3,
            scratch_shapes=[
                *two((3, 2, EXT, LANES)),
                *two((4, N, N)),
                pltpu.VMEM((4, N, N), jnp.float32),
                *two((2 * N, 2 * N), jnp.bfloat16),
                pltpu.VMEM((2, 2, N, LANES), jnp.float32),
                *two((2 * N, 2 * N), jnp.bfloat16),
                pltpu.VMEM((2 * N, 2 * N), jnp.float32),
                pltpu.VMEM((4, 3, 3, 2 * FAR + N, LANES), jnp.float32),
                *two((3, 3, LANES, LANES)),
                *two((3, 3, LANES, LANES)),
                *two((3, 3, BAND, LANES)),
                *two((3, 3, LANES, LANES)),
                *two((3, 3, LANES, LANES)),
                *two((3, BAND, LANES)),
                *two((3, BAND, LANES)),
                *two((blocks, 10, depth, LANES)),
                *two((blocks // 2, 10, depth, LANES)),
                *two((blocks // 2, 10, depth, LANES)),
                *two((nx - 1, ny, 10, depth, LANES)),
                *two((ny, 10, depth, LANES)),
                *two((ny - 1, 10, depth, LANES)),
                *two((zn * nz, depth, LANES)),
                *two((nz - 1, zn, depth, LANES)),
                *two((zn * nz, depth, LANES)),
                *two((blocks, 10, depth, LANES)),
                pltpu.SemaphoreType.DMA((5,)),
                pltpu.SemaphoreType.DMA((COPIES,)),
                pltpu.SemaphoreType.DMA((COPIES,)),
            ],
            compiler_params=pltpu.CompilerParams(
                collective_id=0, has_side_effects=True, vmem_limit_bytes=60 * 1024 * 1024
            ),
            cost_estimate=pl.CostEstimate(
                flops=2 * 4 * 4 * 2 * 512**3, bytes_accessed=6 << 20, transcendentals=8 * N * N
            ),
        )(sample, probe.reshape(4, N, N), amps, table_a, table_b, rows_at, cols_at, live)
        return new_sample, new_probe.reshape(2, 2, N, N), probe_gradient.reshape(2, 2, N, N)

    return jax.shard_map(
        local,
        mesh=mesh,
        in_specs=(
            P(None, "grp", "dev"),
            P(),
            P(("grp", "dev"), None, None),
            P(("grp", "dev")),
            P(("grp", "dev")),
            P(("grp", "dev")),
        ),
        out_specs=(P(None, "grp", "dev"), P(), P()),
        check_vma=False,
    )
```

time: 827 us -> 191 us (0.23)
  waiting for transfers between devices: 606 us -> 0 us
  Pallas kernels: 0 us -> 185 us
  starting transfers between devices: 112 us -> 0 us
  local copies, waits for them, and re-layouts: 48.7 us -> 4.53 us
  other arithmetic: 29.2 us -> 0 us
  between operations: 14.5 us -> 1.3 us
  loops' own time: 8.4 us -> 0 us
    psum x2 -> x0, waiting for transfers between devices: 566 us -> none  [local(): lax.psum((probe_grad, probe_weight), ('grp', 'dev'))]
    pallas_call x0 -> x1, Pallas kernels: none -> 185 us  [local(): pl.pallas_call(functools.partial(kernel, (nx, ny, nz)), out_shape=[jax.Sh...]
    ppermute x16 -> x0, starting transfers between devices: 112 us -> none  [the longest x8 65.6 us: shifted(): return lax.ppermute(x, axis, pairs)]
    ppermute x16 -> x0, waiting for transfers between devices: 39.7 us -> none  [the longest x4 19.7 us: with_halo(): after = lax.ppermute(leading, axis, down)]
    while x7 -> x0, local copies, waits for them, and re-layouts: 16.8 us -> none  [local(): lax.fori_loop(0, capacity, guarded, initial)]
    dynamic_update_slice x2 -> x0, local copies, waits for them, and re-layouts: 15.7 us -> none  [visit_one(): totals = lax.dynamic_update_slice(totals, previous + sample_term, anchor)]
    add x15 -> x0, other arithmetic: 14.6 us -> none  [the longest x2 3.42 us: local(): columns = totals[:, :, margin:margin + tile_cols] + from_next + from_prev]
    another operation x10 -> x0, loops' own time: 8.4 us -> none  [the longest x2 5.37 us: local(): lax.fori_loop(0, capacity, guarded, initial)]
  transfers between devices with their start and end apart: 18 -> 0, of which waited for: 10 -> 0; matrix products, arithmetic and copies ran while one was open for 1% -> 0% of each run, Pallas kernels for 0% -> 0%
where the time goes in v1:
time: 191 us
  Pallas kernels  185 us (97%)
  local copies, waits for them, and re-layouts  4.53 us (2%)
    pallas_call x1, Pallas kernels, local(): pl.pallas_call(functools.partial(kernel, (nx, ny, nz)), out_shape=[jax.Sh...  185 us
    unnamed x7, local copies, waits for them, and re-layouts  4.53 us

profile of v1, /device:TPU:1, one launch (start us, length us, event | category | flops | bytes accessed | tf_op | source)
XLA Modules:
  0.0 191.0 jit_solution(17382555295433123613)
XLA Ops:
  1.3 185.2 %shard_map.103 = (f32[2,512,128]{2,1,0:T(8,128)}, f32[4,256,256]{2,1,0:T(8,128)}, f32[4,256,256]{2,1,0:T(8,128)}) custom-call(f32[2,512,128]{2,1,0:T(8,128)} %sample.1, f32[4,256,256]{2,1,0:T(8,128)} %bitcast.5, f32[4,256,256]{2,1,0:T(8,128)} %amps.1, bf16[512,512]{1,0:T(8,128)(2,1)} %constant.4.clone.table_a, bf16[512,512]{1,0:T(8,128)(2,1)} %constant.5.clone.table_b, ...), custom_call_target="tpu_custom_call" | custom-call | flops 8589934592 | bytes 6291456 | tf_op jit(solution)/shard_map/pallas_call | solution.py:484
  186.5 0.0 copy-start.1
  186.5 2.0 %copy.15 = f32[2,512,128]{2,1,0:T(8,128)} copy(f32[2,512,128]{2,1,0:T(8,128)} %get-tuple-element.12) | data formatting | bytes 1048576
  188.4 0.0 copy-done.1
  188.4 0.0 copy-start
  188.4 1.0 copy.16
  189.4 0.6 copy-done
  190.0 1.0 copy.17
Async XLA Ops:
  186.5 2.0 %copy-start.1 = (f32[4,256,256]{2,1,0:T(8,128)S(1)}, f32[4,256,256]{2,1,0:T(8,128)}, u32[]{:S(2)}) copy-start(f32[4,256,256]{2,1,0:T(8,128)} %get-tuple-element.7) | copy-start | bytes 3145732
  188.4 1.6 copy-start

commit v2 on v0

v2 whole, which is shorter than its diff:
```python
import functools
import math

import jax
import jax.numpy as jnp
import ml_dtypes
import numpy as np
from jax import lax
from jax.experimental import pallas as pl
from jax.experimental.pallas import tpu as pltpu
from jax.sharding import PartitionSpec as P

INTENSITY_FLOOR = 0.25
SAMPLE_DAMPING = 0.5
PROBE_DAMPING = 1.0
MESH = pl.DeviceIdType.MESH
LANES = 128
N = 256
HALF = 128
BAND = 512
EXT = BAND + 2 * LANES
FAR = 512
STEP = 16
SLOTS = 4
COPIES = 176
UP, MIDDLE, DOWN = (0, 128), (128, 384), (384, 512)


def tables():
    k = np.arange(N)
    angles = (np.outer(k, k) % N).astype(np.float32) * np.float32(2.0 * math.pi / N)
    c = (np.cos(angles) / np.float32(16.0)).astype(ml_dtypes.bfloat16)
    s = (np.sin(angles) / np.float32(16.0)).astype(ml_dtypes.bfloat16)
    a = np.block([[c, s], [-s, c]])
    b = np.ascontiguousarray(a.T)

    def blocked(t):
        return np.ascontiguousarray(t.reshape(2, 2, HALF, 2 * N).swapaxes(0, 1).reshape(2 * N, 2 * N))

    return a, b, blocked(a), blocked(b)


def kernel(shape, *refs):
    sample, probe, amps, *table_refs, rows_at, cols_at, live = refs[:10]
    out_sample, out_probe, out_sums, out_weight = refs[10:14]
    scratch = iter(refs[14:])

    def two():
        return next(scratch), next(scratch)

    nx, ny, nz = shape
    field, prb = two(), two()
    amp, ta, tb, la, lb, patch, wave, back, mid, corr, spec, chi, light, placed = (
        next(scratch) for _ in range(14)
    )
    halo_up, halo_dn, own, from_up, from_dn, from_left, from_right = (two() for _ in range(7))
    w_up, w_dn, w_own, w_from_up, w_from_dn, w_left, w_right = (two() for _ in range(7))
    part, rc, hs, rxa, ryb, hxa, hyb, rya, rxb, zb, rz, zg, full = (two() for _ in range(13))
    vpart, vrc, vhs, vrx, vhx, vry, vz, vfull = (two() for _ in range(8))
    load_sem, send_sem, recv_sem = scratch

    g, d = lax.axis_index("grp"), lax.axis_index("dev")
    ng, nd = 2 * ny, nx * nz
    y, core = g // 2, g % 2
    x, z = d // nz, d % nz
    above = {"grp": (g + ng - 1) % ng, "dev": d}
    below = {"grp": (g + 1) % ng, "dev": d}
    left = {"grp": g, "dev": (d + nd - 1) % nd}
    right = {"grp": g, "dev": (d + 1) % nd}
    partner = {"grp": y * 2 + 1 - core, "dev": d}
    xs = [(x + k) % nx for k in range(nx)]
    ys = [(y + k) % ny for k in range(ny)]
    zs = [(z + k) % nz for k in range(nz)]
    on_x = [{"grp": g, "dev": v * nz + z} for v in xs]
    on_y = [{"grp": v * 2 + core, "dev": d} for v in ys]
    on_z = [{"grp": g, "dev": x * nz + v} for v in zs]

    copies = []

    def remote(src, dst, to):
        n = len(copies)
        copy = pltpu.make_async_remote_copy(
            src_ref=src, dst_ref=dst, send_sem=send_sem.at[n], recv_sem=recv_sem.at[n],
            device_id=to, device_id_type=MESH,
        )
        copies.append(copy)
        return copy

    def start(group):
        for copy in group:
            copy.start()
        return group

    def send(src, dst, to):
        return start([remote(src, dst, to)])[0]

    def arrive(group):
        for copy in group:
            copy.wait_recv()

    moves = [(sample, field[0].at[1, :, LANES : LANES + BAND, :]), (probe, prb[0])]
    moves += list(zip(table_refs, (ta, tb, la, lb), strict=True)) + [(amps, amp)]
    loads = [pltpu.make_async_copy(src, dst, load_sem.at[n]) for n, (src, dst) in enumerate(moves)]
    for load in loads:
        load.start()

    barrier = pltpu.get_barrier_semaphore()
    peers = [above, below, left, right, partner] + on_x[1:] + on_y[1:] + on_z[1:]
    for peer in peers:
        pl.semaphore_signal(barrier, inc=1, device_id=peer, device_id_type=MESH)
    pl.semaphore_wait(barrier, len(peers))

    row_anchor = g * BAND - LANES
    col_anchor = d * LANES - LANES
    starts = [jnp.clip(rows_at[p] - row_anchor, 0, FAR) for p in range(SLOTS)]

    def alive(p):
        return jnp.full((STEP, LANES), p, jnp.int32) < jnp.full((STEP, LANES), live[0], jnp.int32)

    def send_columns(f, source, lo, hi):
        src = source(lo, hi)
        return [
            send(src, f.at[0, :, LANES + lo : LANES + hi, :], right),
            send(src, f.at[2, :, LANES + lo : LANES + hi, :], left),
        ]

    def forward_up(f, t, src=None):
        src = f.at[t, :, LANES : 2 * LANES, :] if src is None else src
        return send(src, f.at[t, :, LANES + BAND : EXT, :], above)

    def forward_down(f, t, src=None):
        src = f.at[t, :, BAND : LANES + BAND, :] if src is None else src
        return send(src, f.at[t, :, 0:LANES, :], below)

    def spread(f, sent_up, sent_down, sent_middle, forwards):
        arrive(sent_up)
        forwards += [forward_up(f, 0), forward_up(f, 2)]
        arrive(sent_down)
        forwards += [forward_down(f, 0), forward_down(f, 2)]
        return sent_middle + forwards

    def argument(lo, hi):
        return sample.at[:, lo:hi, :]

    sent_up = send_columns(field[0], argument, *UP)
    sent_down = send_columns(field[0], argument, *DOWN)
    forwards = [forward_up(field[0], 1, argument(*UP)), forward_down(field[0], 1, argument(*DOWN))]
    sent_middle = send_columns(field[0], argument, *MIDDLE)

    def clear(i, _):
        zero = jnp.zeros((STEP, LANES), jnp.float32)
        rr = pl.multiple_of(i * STEP, STEP)
        for p in range(SLOTS):
            for t in range(3):
                for at in (rr, FAR + N + rr):
                    for ch in range(2):
                        placed[p, t, ch, pl.ds(at, STEP), :] = zero
        return 0

    lax.fori_loop(0, FAR // STEP, clear, 0)
    for it in range(2):
        part[it][...] = jnp.zeros(part[it].shape, jnp.float32)
        vpart[it][...] = jnp.zeros(vpart[it].shape, jnp.float32)

    def placing(p):
        s = jnp.clip(cols_at[p] - col_anchor, 0, LANES)
        lane = lax.broadcasted_iota(jnp.int32, (STEP, LANES), 1)
        return s % LANES, lane >= s

    def total(sources, dst, first, lo, hi):
        def body(i, _):
            rr = pl.multiple_of(lo + i * 2 * STEP, 2 * STEP)
            for src, index in sources:
                values = [
                    placed[(p, *src, pl.ds(FAR + first + rr - starts[p], 2 * STEP), slice(None))]
                    for p in range(SLOTS)
                ]
                dst[(*index, pl.ds(rr, 2 * STEP), slice(None))] = (values[0] + values[1]) + (
                    values[2] + values[3]
                )
            return 0

        lax.fori_loop(0, (hi - lo) // (2 * STEP), body, 0)

    grads = [((t, ch), (t, ch)) for t in range(3) for ch in range(2)]
    lights = [((t, 0), (t,)) for t in range(3)]

    def illuminate(it):
        for j in range(2):
            cols = slice(j * LANES, (j + 1) * LANES)
            value = prb[it][0, :, cols] ** 2 + prb[it][1, :, cols] ** 2
            light[j] = value + (prb[it][2, :, cols] ** 2 + prb[it][3, :, cols] ** 2)

        def place(p, _):
            ahead, late = placing(p)
            used = alive(p)
            for rr in range(0, N, STEP):
                a, b = (
                    pltpu.roll(jnp.where(used, light[j, rr : rr + STEP, :], 0.0), ahead, 1) for j in range(2)
                )
                at = slice(FAR + rr, FAR + rr + STEP)
                placed[p, 0, 0, at, :] = jnp.where(late, a, 0.0)
                placed[p, 1, 0, at, :] = jnp.where(late, b, a)
                placed[p, 2, 0, at, :] = jnp.where(late, 0.0, b)
            return 0

        lax.fori_loop(0, SLOTS, place, 0)
        total(lights, w_up[it], 0, 0, LANES)
        up = send(w_up[it], w_from_dn[it], above)
        total(lights, w_dn[it], LANES + BAND, 0, LANES)
        down = send(w_dn[it], w_from_up[it], below)
        total(lights, w_own[it], LANES, 0, BAND)
        return [up, down]

    def gather(it):
        f = field[it]

        def body(p, _):
            r0 = jnp.clip(rows_at[p] - row_anchor, 0, FAR)
            s = jnp.clip(cols_at[p] - col_anchor, 0, LANES)
            behind = (LANES - s) % LANES
            early = lax.broadcasted_iota(jnp.int32, (STEP, LANES), 1) < LANES - s
            used = alive(p)
            for rr in range(0, N, STEP):
                rows = slice(rr, rr + STEP)
                halves = []
                for ch in range(2):
                    a, b, c = (pltpu.roll(f[t, ch, pl.ds(r0 + rr, STEP), :], behind, 1) for t in range(3))
                    halves.append((jnp.where(early, a, b), jnp.where(early, b, c)))
                for j in range(2):
                    o_re, o_im = halves[0][j], halves[1][j]
                    patch[p, 0, j, rows, :] = o_re
                    patch[p, 1, j, rows, :] = o_im
                    v = jnp.where(used, o_re * o_re + o_im * o_im, 0.0).reshape(2, 8, LANES)
                    vpart[it][rr // 8 : rr // 8 + 2, j] += v
            return 0

        lax.fori_loop(0, SLOTS, body, 0)

    def position(it, p):
        pr = prb[it]
        ahead, late = placing(p)
        used = alive(p)
        f32 = jnp.float32
        for rr in range(0, N, STEP):
            rows = slice(rr, rr + STEP)
            low = slice(N + rr, N + rr + STEP)
            for j in range(2):
                o_re, o_im = patch[p, 0, j, rows, :], patch[p, 1, j, rows, :]
                for m in range(2):
                    cols = slice(m * N + j * LANES, m * N + (j + 1) * LANES)
                    p_re = pr[2 * m, rows, j * LANES : (j + 1) * LANES]
                    p_im = pr[2 * m + 1, rows, j * LANES : (j + 1) * LANES]
                    wave[rows, cols] = (p_re * o_re - p_im * o_im).astype(jnp.bfloat16)
                    wave[low, cols] = (p_re * o_im + p_im * o_re).astype(jnp.bfloat16)
        for rb in range(2):
            block = slice(rb * 2 * HALF, (rb + 1) * 2 * HALF)
            first = jnp.dot(la[block, :], wave[...], preferred_element_type=f32).astype(jnp.bfloat16)
            for m in range(2):
                for c in range(2):
                    mid[rb, m * HALF : (m + 1) * HALF, c * N : (c + 1) * N] = first[
                        c * HALF : (c + 1) * HALF, m * N : (m + 1) * N
                    ]
            spec[rb] = jnp.dot(mid[rb], tb[...], preferred_element_type=f32)
            for rr in range(0, HALF, STEP):
                for j in range(2):
                    cols = [slice(c * N + j * LANES, c * N + (j + 1) * LANES) for c in range(2)]
                    rows = [slice(m * HALF + rr, m * HALF + rr + STEP) for m in range(2)]
                    values = [[spec[rb, rows[m], cols[c]] for c in range(2)] for m in range(2)]
                    intensity = (values[0][0] ** 2 + values[0][1] ** 2) + (
                        values[1][0] ** 2 + values[1][1] ** 2
                    )
                    measured = amp[p, rb * HALF + rr : rb * HALF + rr + STEP, cols[0]]
                    factor = measured * lax.rsqrt(jnp.maximum(intensity, INTENSITY_FLOOR)) - 1.0
                    factor = jnp.where(used, factor, 0.0)
                    for m in range(2):
                        for c in range(2):
                            corr[rb, rows[m], cols[c]] = (values[m][c] * factor).astype(jnp.bfloat16)
            undone = jnp.dot(corr[rb], ta[...], preferred_element_type=f32).astype(jnp.bfloat16)
            for m in range(2):
                for c in range(2):
                    back[
                        c * N + rb * HALF : c * N + (rb + 1) * HALF, m * N : (m + 1) * N
                    ] = undone[m * HALF : (m + 1) * HALF, c * N : (c + 1) * N]
        for rb in range(2):
            block = slice(rb * 2 * HALF, (rb + 1) * 2 * HALF)
            chi[rb] = jnp.dot(lb[block, :], back[...], preferred_element_type=f32)
            for rr in range(0, HALF, STEP):
                at = rb * HALF + rr
                rows = slice(at, at + STEP)
                terms = []
                for j in range(2):
                    o_re, o_im = patch[p, 0, j, rows, :], patch[p, 1, j, rows, :]
                    g_re = g_im = 0.0
                    for m in range(2):
                        p_re = pr[2 * m, rows, j * LANES : (j + 1) * LANES]
                        p_im = pr[2 * m + 1, rows, j * LANES : (j + 1) * LANES]
                        cols = slice(m * N + j * LANES, m * N + (j + 1) * LANES)
                        b_re = chi[rb, rr : rr + STEP, cols]
                        b_im = chi[rb, HALF + rr : HALF + rr + STEP, cols]
                        g_re += p_re * b_re + p_im * b_im
                        g_im += p_re * b_im - p_im * b_re
                        h_re = o_re * b_re + o_im * b_im
                        h_im = o_re * b_im - o_im * b_re
                        pair = slice(at // 8, at // 8 + 2)
                        part[it][pair, 4 * m + j] += h_re.reshape(2, 8, LANES)
                        part[it][pair, 4 * m + 2 + j] += h_im.reshape(2, 8, LANES)
                    terms.append((g_re, g_im))
                put = slice(FAR + at, FAR + at + STEP)
                for ch in range(2):
                    a = pltpu.roll(terms[0][ch], ahead, 1)
                    b = pltpu.roll(terms[1][ch], ahead, 1)
                    placed[p, 0, ch, put, :] = jnp.where(late, a, 0.0)
                    placed[p, 1, ch, put, :] = jnp.where(late, b, a)
                    placed[p, 2, ch, put, :] = jnp.where(late, 0.0, b)

    def update(it, lo, hi):
        for rr in range(lo, hi, 2 * STEP):
            rows = slice(rr, rr + 2 * STEP)
            scale = w_own[it][1, rows, :]
            for ch in range(2):
                grad = own[it][1, ch, rows, :] + (from_left[it][ch, rows, :] + from_right[it][ch, rows, :])
                value = field[it][1, ch, LANES + rr : LANES + rr + 2 * STEP, :] + grad * scale
                if it == 0:
                    field[1][1, ch, LANES + rr : LANES + rr + 2 * STEP, :] = value
                else:
                    own[1][1, ch, rows, :] = value
        if it == 1:
            return [write(own[1].at[1, :, lo:hi, :], out_sample.at[:, lo:hi, :])]
        return []

    def finish_probe():
        for i in range(N // 8):
            at = slice(i * 8, i * 8 + 8)
            c, xy = i // (nx * ny), i % (nx * ny)
            for j in range(2):
                cols = slice(j * LANES, (j + 1) * LANES)
                scale = 1.0 / (vfull[0][i, j] + PROBE_DAMPING)
                for q in range(4):
                    grad = full[0][c, xy // ny, xy % ny, 2 * q + j]
                    prb[1][q, at, cols] = prb[0][q, at, cols] + grad * scale

    written = []

    def write(src, dst):
        copy = pltpu.make_async_copy(src, dst, load_sem.at[len(moves) + len(written)])
        copy.start()
        written.append(copy)
        return copy

    flushed = [0]

    def flush():
        for copy in copies[flushed[0] :]:
            copy.wait_send()
        flushed[0] = len(copies)

    for load in loads:
        load.wait()
    rows_w = illuminate(0)
    waiting = spread(field[0], sent_up, sent_down, sent_middle, forwards)
    arrive(waiting)

    half = nx * ny
    for it in range(2):
        if it == 0:
            gather(0)
        else:
            write(prb[1], out_probe)
            rows_w = illuminate(1)

        mine = vfull[it].at[(core * nx + x) * ny + y]
        v_core = remote(vpart[it].at[pl.ds((1 - core) * half, half)], vrc[it], partner)
        v_x = [remote(vhs[it].at[pl.ds(xs[k] * ny, ny)], vrx[it].at[k - 1], on_x[k]) for k in range(1, nx)]
        v_y = [remote(vhx[it].at[ys[k]], vry[it].at[k - 1], on_y[k]) for k in range(1, ny)]
        v_z = [remote(vz[it].at[z], vz[it].at[z], on_z[k]) for k in range(1, nz)]
        v_back_y = [remote(mine, mine, on_y[k]) for k in range(1, ny)]
        row = vfull[it].at[pl.ds((core * nx + x) * ny, ny)]
        v_back_x = [remote(row, row, on_x[k]) for k in range(1, nx)]
        whole = vfull[it].at[pl.ds(core * half, half)]
        v_back_core = remote(whole, whole, partner)
        w_sides = [
            remote(w_own[it].at[0], w_right[it], left),
            remote(w_own[it].at[2], w_left[it], right),
        ]
        v_core.start()

        def weight_core(it=it, v_core=v_core, v_x=v_x):
            v_core.wait_recv()
            vhs[it][...] = vpart[it][pl.ds(core * half, half)] + vrc[it][...]
            start(v_x)

        def weight_x(it=it, v_x=v_x, v_y=v_y):
            arrive(v_x)
            value = vhs[it][pl.ds(x * ny, ny)]
            for k in range(nx - 1):
                value += vrx[it][k]
            vhx[it][...] = value
            start(v_y)

        def light_sides(it=it, rows_w=rows_w, w_sides=w_sides):
            arrive(rows_w)
            for t in range(3):
                w_own[it][t, 0:LANES, :] += w_from_up[it][t]
                w_own[it][t, BAND - LANES : BAND, :] += w_from_dn[it][t]
            start(w_sides)

        def weight_y(it=it, v_y=v_y, v_z=v_z):
            arrive(v_y)
            value = vhx[it][y]
            for k in range(ny - 1):
                value += vry[it][k]
            vz[it][z] = value
            start(v_z)

        def visit(p, _, it=it, hooks=(weight_core, weight_x, light_sides, weight_y)):
            for n, hook in zip((1, 2, 2, 3), hooks, strict=True):
                pl.when(p == n)(hook)
            position(it, p)
            return 0

        lax.fori_loop(0, SLOTS, visit, 0)

        swap = send(part[it].at[pl.ds((1 - core) * half, half)], rc[it], partner)

        total(grads, halo_up[it], 0, 0, LANES)
        rows_up = send(halo_up[it], from_dn[it], above)
        total(grads, halo_dn[it], LANES + BAND, 0, LANES)
        rows_down = send(halo_dn[it], from_up[it], below)

        swap.wait_recv()
        for i in range(nx):
            for j in range(ny):
                hs[it][i, j] = part[it][core * half + i * ny + j] + rc[it][i * ny + j]
        ax = [send(hs[it].at[xs[k], :, 0:4], rxa[it].at[k - 1], on_x[k]) for k in range(1, nx)]
        by = [send(hs[it].at[:, ys[k], 4:8], ryb[it].at[k - 1], on_y[k]) for k in range(1, ny)]

        def send_sides(lo, hi, it=it):
            return [
                send(own[it].at[0, :, lo:hi, :], from_right[it].at[:, lo:hi, :], left),
                send(own[it].at[2, :, lo:hi, :], from_left[it].at[:, lo:hi, :], right),
            ]

        total(grads, own[it], LANES, *MIDDLE)
        side_middle = send_sides(*MIDDLE)

        arrive(v_z)
        value = vz[it][0]
        for k in range(1, nz):
            value += vz[it][k]
        vfull[it][(core * nx + x) * ny + y] = value
        start(v_back_y)

        total(grads, own[it], LANES, *UP)
        total(grads, own[it], LANES, *DOWN)

        def add_rows(src, lo, it=it):
            for t in range(3):
                for ch in range(2):
                    own[it][t, ch, lo : lo + LANES, :] += src[t, ch]

        rows_down.wait_recv()
        add_rows(from_up[it], UP[0])
        side_up = send_sides(*UP)
        rows_up.wait_recv()
        add_rows(from_dn[it], DOWN[0])
        side_down = send_sides(*DOWN)

        arrive(ax)
        value = hs[it][x, :, 0:4]
        for k in range(nx - 1):
            value += rxa[it][k]
        hxa[it][...] = value
        ay = [send(hxa[it].at[ys[k]], rya[it].at[k - 1], on_y[k]) for k in range(1, ny)]
        arrive(by)
        for i in range(nx):
            value = hs[it][i, y, 4:8]
            for k in range(ny - 1):
                value += ryb[it][k, i]
            hyb[it][i] = value
        bx = [send(hyb[it].at[xs[k]], rxb[it].at[k - 1], on_x[k]) for k in range(1, nx)]

        arrive(v_back_y)
        start(v_back_x)

        arrive(w_sides)
        lit = w_own[it][1] + (w_left[it][...] + w_right[it][...])
        w_own[it][1] = 1.0 / (lit + SAMPLE_DAMPING)

        arrive(ay)
        value = hxa[it][y]
        for k in range(ny - 1):
            value += rya[it][k]
        zb[it][0:4] = value
        arrive(bx)
        value = hyb[it][x]
        for k in range(nx - 1):
            value += rxb[it][k]
        zb[it][4:8] = value
        to_z = [send(zb[it].at[zs[k]], rz[it].at[k - 1], on_z[k]) for k in range(1, nz)]

        arrive(v_back_x)
        v_back_core.start()
        if it == 1:
            flush()

        arrive(side_middle)
        update(it, *MIDDLE)

        arrive(to_z)
        value = zb[it][z]
        for k in range(nz - 1):
            value += rz[it][k]
        zg[it][z] = value
        back_z = [send(zg[it].at[z], zg[it].at[z], on_z[k]) for k in range(1, nz)]

        arrive(side_up)
        update(it, *UP)
        if it == 0:

            def updated(lo, hi):
                return field[1].at[1, :, LANES + lo : LANES + hi, :]

            sent_up = send_columns(field[1], updated, *UP)
            forwards = [forward_up(field[1], 1)]

        arrive(back_z)
        full[it][core, x, y] = zg[it][...]
        mine = full[it].at[core, x, y, 0:4]
        ay = [send(mine, mine, on_y[k]) for k in range(1, ny)]
        mine = full[it].at[core, x, y, 4:8]
        bx = [send(mine, mine, on_x[k]) for k in range(1, nx)]

        arrive(side_down)
        update(it, *DOWN)
        if it == 0:
            sent_down = send_columns(field[1], updated, *DOWN)
            forwards.append(forward_down(field[1], 1))
            sent_middle = send_columns(field[1], updated, *MIDDLE)

        arrive(ay)
        mine = full[it].at[core, x, :, 0:4]
        ax = [send(mine, mine, on_x[k]) for k in range(1, nx)]
        arrive(bx)
        mine = full[it].at[core, :, y, 4:8]
        by = [send(mine, mine, on_y[k]) for k in range(1, ny)]
        if it == 0:
            waiting = spread(field[1], sent_up, sent_down, sent_middle, forwards)
        arrive(ax)
        arrive(by)
        mine = full[it].at[core]
        back_core = send(mine, mine, partner)
        v_back_core.wait_recv()
        if it == 0:
            arrive(waiting)
            gather(1)
            back_core.wait_recv()
            finish_probe()
        else:
            write(vfull[1], out_weight)
            flush()
            back_core.wait_recv()
            write(full[1], out_sums)

    for copy in written:
        copy.wait()


def finish(scale, sample, probe, sums, weight, new_sample, new_probe, probe_gradient):
    new_sample[...] = sample[...]
    for b in range(sums.shape[0]):
        rows = slice(8 * b, 8 * b + 8)
        for j in range(2):
            cols = slice(j * LANES, (j + 1) * LANES)
            damped = 1.0 / (weight[b, j] + PROBE_DAMPING)
            for q in range(4):
                grad = sums[b, 2 * q + j]
                new_probe[q // 2, q % 2, rows, cols] = probe[q, rows, cols] + grad * damped
                probe_gradient[q // 2, q % 2, rows, cols] = grad * scale


def solution(mesh):
    ng, nd = mesh.shape["grp"], mesh.shape["dev"]
    ny = ng // 2
    nz = nd // 4
    nx = nd // nz
    blocks = 2 * nx * ny
    args = tables()

    def vmem(*shape, dtype=jnp.float32):
        return pltpu.VMEM(shape, dtype)

    def two(*shape):
        return [vmem(*shape)] * 2

    def local(sample, probe, amps, rows_at, cols_at, live):
        hbm = pl.BlockSpec(memory_space=pl.ANY)
        smem = pl.BlockSpec(memory_space=pltpu.SMEM)
        square = (2 * N, 2 * N)
        f32 = jnp.float32
        raw_sample, raw_probe, sums, weight = pl.pallas_call(
            functools.partial(kernel, (nx, ny, nz)),
            out_shape=[
                jax.ShapeDtypeStruct((2, BAND, LANES), f32),
                jax.ShapeDtypeStruct((4, N, N), f32),
                jax.ShapeDtypeStruct((2, nx, ny, 8, 8, LANES), f32),
                jax.ShapeDtypeStruct((blocks, 2, 8, LANES), f32),
            ],
            in_specs=[hbm] * 7 + [smem] * 3,
            out_specs=[hbm] * 4,
            scratch_shapes=[
                *two(3, 2, EXT, LANES),
                *two(4, N, N),
                vmem(SLOTS, N, N),
                *[vmem(*square, dtype=jnp.bfloat16)] * 4,
                vmem(SLOTS, 2, 2, N, LANES),
                *[vmem(*square, dtype=jnp.bfloat16)] * 2,
                *[vmem(2, 2 * HALF, 2 * N, dtype=jnp.bfloat16)] * 2,
                *[vmem(2, 2 * HALF, 2 * N)] * 2,
                vmem(2, N, LANES),
                vmem(SLOTS, 3, 2, 2 * FAR + N, LANES),
                *two(3, 2, LANES, LANES),
                *two(3, 2, LANES, LANES),
                *two(3, 2, BAND, LANES),
                *two(3, 2, LANES, LANES),
                *two(3, 2, LANES, LANES),
                *two(2, BAND, LANES),
                *two(2, BAND, LANES),
                *two(3, LANES, LANES),
                *two(3, LANES, LANES),
                *two(3, BAND, LANES),
                *two(3, LANES, LANES),
                *two(3, LANES, LANES),
                *two(BAND, LANES),
                *two(BAND, LANES),
                *two(blocks, 8, 8, LANES),
                *two(blocks // 2, 8, 8, LANES),
                *two(nx, ny, 8, 8, LANES),
                *two(nx - 1, ny, 4, 8, LANES),
                *two(ny - 1, nx, 4, 8, LANES),
                *two(ny, 4, 8, LANES),
                *two(nx, 4, 8, LANES),
                *two(ny - 1, 4, 8, LANES),
                *two(nx - 1, 4, 8, LANES),
                *two(8, 8, LANES),
                *two(nz - 1, 8, LANES),
                *two(8, 8, LANES),
                *two(2, nx, ny, 8, 8, LANES),
                *two(blocks, 2, 8, LANES),
                *two(blocks // 2, 2, 8, LANES),
                *two(blocks // 2, 2, 8, LANES),
                *two(nx - 1, ny, 2, 8, LANES),
                *two(ny, 2, 8, LANES),
                *two(ny - 1, 2, 8, LANES),
                *two(nz, 2, 8, LANES),
                *two(blocks, 2, 8, LANES),
                pltpu.SemaphoreType.DMA((13,)),
                pltpu.SemaphoreType.DMA((COPIES,)),
                pltpu.SemaphoreType.DMA((COPIES,)),
            ],
            compiler_params=pltpu.CompilerParams(
                collective_id=0, has_side_effects=True, vmem_limit_bytes=60 * 1024 * 1024
            ),
            cost_estimate=pl.CostEstimate(
                flops=2 * 4 * 4 * 2 * 512**3, bytes_accessed=6 << 20, transcendentals=8 * N * N
            ),
        )(sample, probe.reshape(4, N, N), amps, *args, rows_at, cols_at, live)
        steps = 4
        some, rows = blocks // steps, N // steps
        tile = pl.BlockSpec((2, BAND // steps, LANES), lambda i: (0, i, 0))
        modes = pl.BlockSpec((2, 2, rows, N), lambda i: (0, 0, i, 0))
        return pl.pallas_call(
            functools.partial(finish, 1.0 / math.sqrt(SLOTS * ng * nd)),
            grid=(steps,),
            out_shape=[
                jax.ShapeDtypeStruct((2, BAND, LANES), f32),
                jax.ShapeDtypeStruct((2, 2, N, N), f32),
                jax.ShapeDtypeStruct((2, 2, N, N), f32),
            ],
            in_specs=[
                tile,
                pl.BlockSpec((4, rows, N), lambda i: (0, i, 0)),
                pl.BlockSpec((some, 8, 8, LANES), lambda i: (i, 0, 0, 0)),
                pl.BlockSpec((some, 2, 8, LANES), lambda i: (i, 0, 0, 0)),
            ],
            out_specs=[tile, modes, modes],
            compiler_params=pltpu.CompilerParams(vmem_limit_bytes=60 * 1024 * 1024),
            cost_estimate=pl.CostEstimate(flops=16 * N * N, bytes_accessed=6 << 20, transcendentals=0),
        )(raw_sample, raw_probe, sums.reshape(blocks, 8, 8, LANES), weight)

    return jax.shard_map(
        local,
        mesh=mesh,
        in_specs=(
            P(None, "grp", "dev"),
            P(),
            P(("grp", "dev"), None, None),
            P(("grp", "dev")),
            P(("grp", "dev")),
            P(("grp", "dev")),
        ),
        out_specs=(P(None, "grp", "dev"), P(), P()),
        check_vma=False,
    )
```

time: 827 us -> 153 us (0.19)
  waiting for transfers between devices: 606 us -> 0 us
  Pallas kernels: 0 us -> 152 us
  starting transfers between devices: 112 us -> 0 us
  local copies, waits for them, and re-layouts: 48.7 us -> 0 us
  other arithmetic: 29.2 us -> 0 us
  between operations: 14.5 us -> 1.29 us
  loops' own time: 8.4 us -> 0 us
    psum x2 -> x0, waiting for transfers between devices: 566 us -> none  [local(): lax.psum((probe_grad, probe_weight), ('grp', 'dev'))]
    pallas_call x0 -> x2, Pallas kernels: none -> 152 us  [the longest x1 148 us: local(): pl.pallas_call(functools.partial(kernel, (nx, ny, nz)), out_shape=[jax.Sh...]
    ppermute x16 -> x0, starting transfers between devices: 112 us -> none  [the longest x8 65.6 us: shifted(): return lax.ppermute(x, axis, pairs)]
    ppermute x16 -> x0, waiting for transfers between devices: 39.7 us -> none  [the longest x4 19.7 us: with_halo(): after = lax.ppermute(leading, axis, down)]
    while x7 -> x0, local copies, waits for them, and re-layouts: 16.8 us -> none  [local(): lax.fori_loop(0, capacity, guarded, initial)]
    dynamic_update_slice x2 -> x0, local copies, waits for them, and re-layouts: 15.7 us -> none  [visit_one(): totals = lax.dynamic_update_slice(totals, previous + sample_term, anchor)]
    add x15 -> x0, other arithmetic: 14.6 us -> none  [the longest x2 3.42 us: local(): columns = totals[:, :, margin:margin + tile_cols] + from_next + from_prev]
    another operation x10 -> x0, loops' own time: 8.4 us -> none  [the longest x2 5.37 us: local(): lax.fori_loop(0, capacity, guarded, initial)]
  transfers between devices with their start and end apart: 18 -> 0, of which waited for: 10 -> 0; matrix products, arithmetic and copies ran while one was open for 1% -> 0% of each run, Pallas kernels for 0% -> 0%
where the time goes in v2:
time: 153 us
  Pallas kernels  152 us (99%)
    pallas_call x1, Pallas kernels, local(): pl.pallas_call(functools.partial(kernel, (nx, ny, nz)), out_shape=[jax.Sh...  148 us
    pallas_call x1, Pallas kernels, local(): pl.pallas_call(functools.partial(finish, 1.0 / math.sqrt(SLOTS * ng * nd)...  4.01 us

profile of v2, /device:TPU:1, one launch (start us, length us, event | category | flops | bytes accessed | tf_op | source)
XLA Modules:
  0.0 153.2 jit_solution(13815732290034032306)
XLA Ops:
  1.3 147.9 %shard_map.121 = (f32[2,512,128]{2,1,0:T(8,128)}, f32[4,256,256]{2,1,0:T(8,128)}, f32[2,4,4,8,8,128]{5,4,3,2,1,0:T(8,128)}, f32[32,2,8,128]{3,2,1,0:T(8,128)}) custom-call(f32[2,512,128]{2,1,0:T(8,128)} %refs_0_.1, f32[4,256,256]{2,1,0:T(8,128)} %bitcast.3, f32[4,256,256]{2,1,0:T(8,128)} %refs_2_.1, bf16[512,512]{1,0:T(8,128)(2,1)} %constant.8.clone.refs_3_, ...), custom_call_target="tpu_custom_call" | custom-call | flops 8589934592 | bytes 6291456 | tf_op jit(solution)/shard_map/pallas_call | solution.py:601
  149.1 4.0 %shard_map.122 = (f32[2,512,128]{2,1,0:T(8,128)}, f32[2,2,256,256]{3,2,1,0:T(8,128)}, f32[2,2,256,256]{3,2,1,0:T(8,128)}) custom-call(f32[2,512,128]{2,1,0:T(8,128)} %get-tuple-element.7.sample, f32[4,256,256]{2,1,0:T(8,128)} %get-tuple-element.8.probe, f32[32,8,8,128]{3,2,1,0:T(8,128)} %bitcast.2, f32[32,2,8,128]{3,2,1,0:T(8,128)} %get-tuple-element.10.weight), custom_call_target="tpu_custom_call" | custom-call | flops 1048576 | bytes 6291456 | tf_op jit(solution)/shard_map/pallas_call | solution.py:672

commit v3 on v2

--- a/solution.py
+++ b/solution.py
@@ -22,7 +22,7 @@
 FAR = 512
 STEP = 16
 SLOTS = 4
-COPIES = 176
+COPIES = 192
 UP, MIDDLE, DOWN = (0, 128), (128, 384), (384, 512)
 
 
@@ -55,7 +55,7 @@
     )
     halo_up, halo_dn, own, from_up, from_dn, from_left, from_right = (two() for _ in range(7))
     w_up, w_dn, w_own, w_from_up, w_from_dn, w_left, w_right = (two() for _ in range(7))
-    part, rc, hs, rxa, ryb, hxa, hyb, rya, rxb, zb, rz, zg, full = (two() for _ in range(13))
+    part, rc, hs, r1, r2, hy, rx, zb, rz, zg, full = (two() for _ in range(11))
     vpart, vrc, vhs, vrx, vhx, vry, vz, vfull = (two() for _ in range(8))
     load_sem, send_sem, recv_sem = scratch
 
@@ -302,9 +302,10 @@
                         g_im += p_re * b_im - p_im * b_re
                         h_re = o_re * b_re + o_im * b_im
                         h_im = o_re * b_im - o_im * b_re
-                        pair = slice(at // 8, at // 8 + 2)
-                        part[it][pair, 4 * m + j] += h_re.reshape(2, 8, LANES)
-                        part[it][pair, 4 * m + 2 + j] += h_im.reshape(2, 8, LANES)
+                        b = at // 8
+                        pair = (b // (nx * ny), b // ny % nx, slice(b % ny, b % ny + 2))
+                        part[it][(*pair, 4 * m + j)] += h_re.reshape(2, 8, LANES)
+                        part[it][(*pair, 4 * m + 2 + j)] += h_im.reshape(2, 8, LANES)
                     terms.append((g_re, g_im))
                 put = slice(FAR + at, FAR + at + STEP)
                 for ch in range(2):
@@ -421,19 +422,29 @@
 
         lax.fori_loop(0, SLOTS, visit, 0)
 
-        swap = send(part[it].at[pl.ds((1 - core) * half, half)], rc[it], partner)
+        sums, mates = part[it], rc[it]
+        order = (2, 1, 3, 0)
+        swap = [send(sums.at[1 - core, :, ys[k]], mates.at[:, ys[k]], partner) for k in order]
+        planes = [slice(4 * h, 4 * h + 4) for h in range(2)]
 
         total(grads, halo_up[it], 0, 0, LANES)
         rows_up = send(halo_up[it], from_dn[it], above)
         total(grads, halo_dn[it], LANES + BAND, 0, LANES)
         rows_down = send(halo_dn[it], from_up[it], below)
 
-        swap.wait_recv()
-        for i in range(nx):
-            for j in range(ny):
-                hs[it][i, j] = part[it][core * half + i * ny + j] + rc[it][i * ny + j]
-        ax = [send(hs[it].at[xs[k], :, 0:4], rxa[it].at[k - 1], on_x[k]) for k in range(1, nx)]
-        by = [send(hs[it].at[:, ys[k], 4:8], ryb[it].at[k - 1], on_y[k]) for k in range(1, ny)]
+        def sum_core(n, it=it, swap=swap):
+            swap[n].wait_recv()
+            at = ys[order[n]]
+            hs[it][:, at] = part[it][core, :, at] + rc[it][:, at]
+
+        sum_core(0)
+        far = [
+            [
+                send(hs[it].at[0:2, ys[2], p], r1[it].at[0, h], on_y[1]),
+                send(hs[it].at[2:4, ys[2], p], r1[it].at[1, h], on_y[3]),
+            ]
+            for h, p in enumerate(planes)
+        ]
 
         def send_sides(lo, hi, it=it):
             return [
@@ -443,6 +454,42 @@
 
         total(grads, own[it], LANES, *MIDDLE)
         side_middle = send_sides(*MIDDLE)
+
+        sum_core(1)
+        sum_core(2)
+        near = []
+        for h, p in enumerate(planes):
+            arrive(far[h])
+            hs[it][0:2, ys[1], p] += r1[it][0, h]
+            hs[it][2:4, ys[3], p] += r1[it][1, h]
+            near.append(
+                [
+                    send(hs[it].at[:, ys[1], p], r2[it].at[0, h], on_y[1]),
+                    send(hs[it].at[:, ys[3], p], r2[it].at[1, h], on_y[3]),
+                ]
+            )
+        sum_core(3)
+
+        total(grads, own[it], LANES, *UP)
+        total(grads, own[it], LANES, *DOWN)
+
+        def add_rows(src, lo, it=it):
+            for t in range(3):
+                for ch in range(2):
+                    own[it][t, ch, lo : lo + LANES, :] += src[t, ch]
+
+        rows_down.wait_recv()
+        add_rows(from_up[it], UP[0])
+        side_up = send_sides(*UP)
+        rows_up.wait_recv()
+        add_rows(from_dn[it], DOWN[0])
+        side_down = send_sides(*DOWN)
+
+        to_x = []
+        for h, p in enumerate(planes):
+            arrive(near[h])
+            hy[it][h] = hs[it][:, y, p] + (r2[it][0, h] + r2[it][1, h])
+            to_x.append([send(hy[it].at[h, xs[k]], rx[it].at[h, k - 1], on_x[k]) for k in range(1, nx)])
 
         arrive(v_z)
         value = vz[it][0]
@@ -451,58 +498,20 @@
         vfull[it][(core * nx + x) * ny + y] = value
         start(v_back_y)
 
-        total(grads, own[it], LANES, *UP)
-        total(grads, own[it], LANES, *DOWN)
-
-        def add_rows(src, lo, it=it):
-            for t in range(3):
-                for ch in range(2):
-                    own[it][t, ch, lo : lo + LANES, :] += src[t, ch]
-
-        rows_down.wait_recv()
-        add_rows(from_up[it], UP[0])
-        side_up = send_sides(*UP)
-        rows_up.wait_recv()
-        add_rows(from_dn[it], DOWN[0])
-        side_down = send_sides(*DOWN)
-
-        arrive(ax)
-        value = hs[it][x, :, 0:4]
-        for k in range(nx - 1):
-            value += rxa[it][k]
-        hxa[it][...] = value
-        ay = [send(hxa[it].at[ys[k]], rya[it].at[k - 1], on_y[k]) for k in range(1, ny)]
-        arrive(by)
-        for i in range(nx):
-            value = hs[it][i, y, 4:8]
-            for k in range(ny - 1):
-                value += ryb[it][k, i]
-            hyb[it][i] = value
-        bx = [send(hyb[it].at[xs[k]], rxb[it].at[k - 1], on_x[k]) for k in range(1, nx)]
-
-        arrive(v_back_y)
-        start(v_back_x)
-
         arrive(w_sides)
         lit = w_own[it][1] + (w_left[it][...] + w_right[it][...])
         w_own[it][1] = 1.0 / (lit + SAMPLE_DAMPING)
 
-        arrive(ay)
-        value = hxa[it][y]
-        for k in range(ny - 1):
-            value += rya[it][k]
-        zb[it][0:4] = value
-        arrive(bx)
-        value = hyb[it][x]
-        for k in range(nx - 1):
-            value += rxb[it][k]
-        zb[it][4:8] = value
+        for h, p in enumerate(planes):
+            arrive(to_x[h])
+            value = hy[it][h, x]
+            for k in range(nx - 1):
+                value += rx[it][h, k]
+            zb[it][p] = value
         to_z = [send(zb[it].at[zs[k]], rz[it].at[k - 1], on_z[k]) for k in range(1, nz)]
 
-        arrive(v_back_x)
-        v_back_core.start()
-        if it == 1:
-            flush()
+        arrive(v_back_y)
+        start(v_back_x)
 
         arrive(side_middle)
         update(it, *MIDDLE)
@@ -525,11 +534,14 @@
             forwards = [forward_up(field[1], 1)]
 
         arrive(back_z)
-        full[it][core, x, y] = zg[it][...]
-        mine = full[it].at[core, x, y, 0:4]
-        ay = [send(mine, mine, on_y[k]) for k in range(1, ny)]
-        mine = full[it].at[core, x, y, 4:8]
-        bx = [send(mine, mine, on_x[k]) for k in range(1, nx)]
+        result = full[it]
+        result[core, x, y] = zg[it][...]
+        mine = [result.at[core, x, y, p] for p in planes]
+        back_x = [[send(m, m, on_x[k]) for k in range(1, nx)] for m in mine]
+        arrive(v_back_x)
+        v_back_core.start()
+        if it == 1:
+            flush()
 
         arrive(side_down)
         update(it, *DOWN)
@@ -538,28 +550,37 @@
             forwards.append(forward_down(field[1], 1))
             sent_middle = send_columns(field[1], updated, *MIDDLE)
 
-        arrive(ay)
-        mine = full[it].at[core, x, :, 0:4]
-        ax = [send(mine, mine, on_x[k]) for k in range(1, nx)]
-        arrive(bx)
-        mine = full[it].at[core, :, y, 4:8]
-        by = [send(mine, mine, on_y[k]) for k in range(1, ny)]
+        def to_core(k, result=result):
+            piece = result.at[core, :, ys[k]]
+            return send(piece, piece, partner)
+
+        back_near = []
+        for h, p in enumerate(planes):
+            arrive(back_x[h])
+            mine = result.at[core, :, y, p]
+            back_near.append([send(mine, mine, on_y[k]) for k in (1, 3)])
+        back_core = [to_core(0)]
+        back_far = []
+        for h, p in enumerate(planes):
+            arrive(back_near[h])
+            low, high = result.at[core, 0:2, ys[3], p], result.at[core, 2:4, ys[1], p]
+            back_far.append([send(low, low, on_y[1]), send(high, high, on_y[3])])
+        back_core += [to_core(1), to_core(3)]
         if it == 0:
             waiting = spread(field[1], sent_up, sent_down, sent_middle, forwards)
-        arrive(ax)
-        arrive(by)
-        mine = full[it].at[core]
-        back_core = send(mine, mine, partner)
+        for h in range(2):
+            arrive(back_far[h])
+        back_core.append(to_core(2))
         v_back_core.wait_recv()
         if it == 0:
             arrive(waiting)
             gather(1)
-            back_core.wait_recv()
+            arrive(back_core)
             finish_probe()
         else:
             write(vfull[1], out_weight)
             flush()
-            back_core.wait_recv()
+            arrive(back_core)
             write(full[1], out_sums)
 
     for copy in written:
@@ -633,15 +654,13 @@
                 *two(3, LANES, LANES),
                 *two(BAND, LANES),
                 *two(BAND, LANES),
-                *two(blocks, 8, 8, LANES),
-                *two(blocks // 2, 8, 8, LANES),
+                *two(2, nx, ny, 8, 8, LANES),
                 *two(nx, ny, 8, 8, LANES),
-                *two(nx - 1, ny, 4, 8, LANES),
-                *two(ny - 1, nx, 4, 8, LANES),
-                *two(ny, 4, 8, LANES),
-                *two(nx, 4, 8, LANES),
-                *two(ny - 1, 4, 8, LANES),
-                *two(nx - 1, 4, 8, LANES),
+                *two(nx, ny, 8, 8, LANES),
+                *two(2, 2, nx // 2, 4, 8, LANES),
+                *two(2, 2, nx, 4, 8, LANES),
+                *two(2, nx, 4, 8, LANES),
+                *two(2, nx - 1, 4, 8, LANES),
                 *two(8, 8, LANES),
                 *two(nz - 1, 8, LANES),
                 *two(8, 8, LANES),

time: 153 us -> 150 us (0.980)
  Pallas kernels: 152 us -> 149 us
    pallas_call x1, Pallas kernels: 148 us -> 145 us  [local(): pl.pallas_call(functools.partial(kernel, (nx, ny, nz)), out_shape=[jax.Sh...]
where the time goes in v3:
time: 150 us
  Pallas kernels  149 us (99%)
    pallas_call x1, Pallas kernels, local(): pl.pallas_call(functools.partial(kernel, (nx, ny, nz)), out_shape=[jax.Sh...  145 us
    pallas_call x1, Pallas kernels, local(): pl.pallas_call(functools.partial(finish, 1.0 / math.sqrt(SLOTS * ng * nd)...  4.01 us

profile of v3, /device:TPU:1, one launch (start us, length us, event | category | flops | bytes accessed | tf_op | source)
XLA Modules:
  0.0 150.2 jit_solution(13483653682659832284)
XLA Ops:
  1.3 144.9 %shard_map.121 = (f32[2,512,128]{2,1,0:T(8,128)}, f32[4,256,256]{2,1,0:T(8,128)}, f32[2,4,4,8,8,128]{5,4,3,2,1,0:T(8,128)}, f32[32,2,8,128]{3,2,1,0:T(8,128)}) custom-call(f32[2,512,128]{2,1,0:T(8,128)} %refs_0_.1, f32[4,256,256]{2,1,0:T(8,128)} %bitcast.3, f32[4,256,256]{2,1,0:T(8,128)} %refs_2_.1, bf16[512,512]{1,0:T(8,128)(2,1)} %constant.8.clone.refs_3_, ...), custom_call_target="tpu_custom_call" | custom-call | flops 8589934592 | bytes 6291456 | tf_op jit(solution)/shard_map/pallas_call | solution.py:622
  146.2 4.0 %shard_map.122 = (f32[2,512,128]{2,1,0:T(8,128)}, f32[2,2,256,256]{3,2,1,0:T(8,128)}, f32[2,2,256,256]{3,2,1,0:T(8,128)}) custom-call(f32[2,512,128]{2,1,0:T(8,128)} %get-tuple-element.7.sample, f32[4,256,256]{2,1,0:T(8,128)} %get-tuple-element.8.probe, f32[32,8,8,128]{3,2,1,0:T(8,128)} %bitcast.2, f32[32,2,8,128]{3,2,1,0:T(8,128)} %get-tuple-element.10.weight), custom_call_target="tpu_custom_call" | custom-call | flops 1048576 | bytes 6291456 | tf_op jit(solution)/shard_map/pallas_call | solution.py:691

commit v4 on v3

--- a/solution.py
+++ b/solution.py
@@ -31,27 +31,23 @@
     angles = (np.outer(k, k) % N).astype(np.float32) * np.float32(2.0 * math.pi / N)
     c = (np.cos(angles) / np.float32(16.0)).astype(ml_dtypes.bfloat16)
     s = (np.sin(angles) / np.float32(16.0)).astype(ml_dtypes.bfloat16)
-    a = np.block([[c, s], [-s, c]])
-    b = np.ascontiguousarray(a.T)
-
-    def blocked(t):
-        return np.ascontiguousarray(t.reshape(2, 2, HALF, 2 * N).swapaxes(0, 1).reshape(2 * N, 2 * N))
-
-    return a, b, blocked(a), blocked(b)
+    split = [np.block([[c[e::2, :HALF], s[e::2, :HALF]], [-s[e::2, :HALF], c[e::2, :HALF]]]) for e in range(2)]
+    order = np.eye(N)[np.concatenate([k[0::2], k[1::2]])].astype(ml_dtypes.bfloat16)
+    return np.stack([*split, split[0].T, split[1].T, order, order.T])
 
 
 def kernel(shape, *refs):
-    sample, probe, amps, *table_refs, rows_at, cols_at, live = refs[:10]
-    out_sample, out_probe, out_sums, out_weight = refs[10:14]
-    scratch = iter(refs[14:])
+    sample, probe, amps, table, rows_at, cols_at, live = refs[:7]
+    out_sample, out_probe, out_sums, out_weight = refs[7:11]
+    scratch = iter(refs[11:])
 
     def two():
         return next(scratch), next(scratch)
 
     nx, ny, nz = shape
     field, prb = two(), two()
-    amp, ta, tb, la, lb, patch, wave, back, mid, corr, spec, chi, light, placed = (
-        next(scratch) for _ in range(14)
+    amp, tab, patch, wave, back, mid, corr, done, spec, undone, chi, light, placed = (
+        next(scratch) for _ in range(13)
     )
     halo_up, halo_dn, own, from_up, from_dn, from_left, from_right = (two() for _ in range(7))
     w_up, w_dn, w_own, w_from_up, w_from_dn, w_left, w_right = (two() for _ in range(7))
@@ -98,8 +94,7 @@
         for copy in group:
             copy.wait_recv()
 
-    moves = [(sample, field[0].at[1, :, LANES : LANES + BAND, :]), (probe, prb[0])]
-    moves += list(zip(table_refs, (ta, tb, la, lb), strict=True)) + [(amps, amp)]
+    moves = [(sample, field[0].at[1, :, LANES : LANES + BAND, :]), (probe, prb[0]), (table, tab), (amps, amp)]
     loads = [pltpu.make_async_copy(src, dst, load_sem.at[n]) for n, (src, dst) in enumerate(moves)]
     for load in loads:
         load.start()
@@ -237,67 +232,97 @@
 
         lax.fori_loop(0, SLOTS, body, 0)
 
+    def order_amplitudes(p, _):
+        rest = amp[p]
+        total_of = None
+        for _ in range(3):
+            bits = rest.astype(jnp.bfloat16)
+            rest = rest - bits.astype(jnp.float32)
+            rows = jnp.dot(tab[4], bits, preferred_element_type=jnp.float32).astype(jnp.bfloat16)
+            moved = jnp.dot(rows, tab[5], preferred_element_type=jnp.float32)
+            total_of = moved if total_of is None else total_of + moved
+        amp[p] = total_of
+        return 0
+
     def position(it, p):
         pr = prb[it]
         ahead, late = placing(p)
         used = alive(p)
-        f32 = jnp.float32
-        for rr in range(0, N, STEP):
-            rows = slice(rr, rr + STEP)
-            low = slice(N + rr, N + rr + STEP)
-            for j in range(2):
-                o_re, o_im = patch[p, 0, j, rows, :], patch[p, 1, j, rows, :]
-                for m in range(2):
-                    cols = slice(m * N + j * LANES, m * N + (j + 1) * LANES)
-                    p_re = pr[2 * m, rows, j * LANES : (j + 1) * LANES]
-                    p_im = pr[2 * m + 1, rows, j * LANES : (j + 1) * LANES]
-                    wave[rows, cols] = (p_re * o_re - p_im * o_im).astype(jnp.bfloat16)
-                    wave[low, cols] = (p_re * o_im + p_im * o_re).astype(jnp.bfloat16)
-        for rb in range(2):
-            block = slice(rb * 2 * HALF, (rb + 1) * 2 * HALF)
-            first = jnp.dot(la[block, :], wave[...], preferred_element_type=f32).astype(jnp.bfloat16)
-            for m in range(2):
-                for c in range(2):
-                    mid[rb, m * HALF : (m + 1) * HALF, c * N : (c + 1) * N] = first[
-                        c * HALF : (c + 1) * HALF, m * N : (m + 1) * N
-                    ]
-            spec[rb] = jnp.dot(mid[rb], tb[...], preferred_element_type=f32)
+        f32, bf16 = jnp.float32, jnp.bfloat16
+        halves = range(2)
+
+        def lanes(first, j):
+            return slice(first + j * LANES, first + (j + 1) * LANES)
+
+        for rr in range(0, HALF, STEP):
+            for j in halves:
+                for m in halves:
+                    both = []
+                    for e in halves:
+                        rows = slice(e * HALF + rr, e * HALF + rr + STEP)
+                        o_re, o_im = patch[p, 0, j, rows, :], patch[p, 1, j, rows, :]
+                        p_re, p_im = pr[2 * m, rows, lanes(0, j)], pr[2 * m + 1, rows, lanes(0, j)]
+                        both.append((p_re * o_re - p_im * o_im, p_re * o_im + p_im * o_re))
+                    for c in halves:
+                        rows = slice(c * HALF + rr, c * HALF + rr + STEP)
+                        wave[0, rows, lanes(m * N, j)] = (both[0][c] + both[1][c]).astype(bf16)
+                        wave[1, rows, lanes(m * N, j)] = (both[0][c] - both[1][c]).astype(bf16)
+        for e in halves:
+            done[e] = jnp.dot(tab[e], wave[e], preferred_element_type=f32)
+        for e in halves:
             for rr in range(0, HALF, STEP):
-                for j in range(2):
-                    cols = [slice(c * N + j * LANES, c * N + (j + 1) * LANES) for c in range(2)]
-                    rows = [slice(m * HALF + rr, m * HALF + rr + STEP) for m in range(2)]
-                    values = [[spec[rb, rows[m], cols[c]] for c in range(2)] for m in range(2)]
+                for m in halves:
+                    for c in halves:
+                        rows = slice(c * HALF + rr, c * HALF + rr + STEP)
+                        a, b = done[e, rows, lanes(m * N, 0)], done[e, rows, lanes(m * N, 1)]
+                        rows = slice(m * HALF + rr, m * HALF + rr + STEP)
+                        mid[e, 0, rows, lanes(0, c)] = (a + b).astype(bf16)
+                        mid[e, 1, rows, lanes(0, c)] = (a - b).astype(bf16)
+            for o in halves:
+                spec[e, o] = jnp.dot(mid[e, o], tab[2 + o], preferred_element_type=f32)
+            for o in halves:
+                for rr in range(0, HALF, STEP):
+                    rows = [slice(m * HALF + rr, m * HALF + rr + STEP) for m in halves]
+                    values = [[spec[e, o, rows[m], lanes(0, c)] for c in halves] for m in halves]
                     intensity = (values[0][0] ** 2 + values[0][1] ** 2) + (
                         values[1][0] ** 2 + values[1][1] ** 2
                     )
-                    measured = amp[p, rb * HALF + rr : rb * HALF + rr + STEP, cols[0]]
+                    measured = amp[p, e * HALF + rr : e * HALF + rr + STEP, lanes(0, o)]
                     factor = measured * lax.rsqrt(jnp.maximum(intensity, INTENSITY_FLOOR)) - 1.0
                     factor = jnp.where(used, factor, 0.0)
-                    for m in range(2):
-                        for c in range(2):
-                            corr[rb, rows[m], cols[c]] = (values[m][c] * factor).astype(jnp.bfloat16)
-            undone = jnp.dot(corr[rb], ta[...], preferred_element_type=f32).astype(jnp.bfloat16)
-            for m in range(2):
-                for c in range(2):
-                    back[
-                        c * N + rb * HALF : c * N + (rb + 1) * HALF, m * N : (m + 1) * N
-                    ] = undone[m * HALF : (m + 1) * HALF, c * N : (c + 1) * N]
-        for rb in range(2):
-            block = slice(rb * 2 * HALF, (rb + 1) * 2 * HALF)
-            chi[rb] = jnp.dot(lb[block, :], back[...], preferred_element_type=f32)
+                    for m in halves:
+                        for c in halves:
+                            corr[e, o, rows[m], lanes(0, c)] = (values[m][c] * factor).astype(bf16)
+            for o in halves:
+                undone[e, o] = jnp.dot(corr[e, o], tab[o], preferred_element_type=f32)
             for rr in range(0, HALF, STEP):
-                at = rb * HALF + rr
-                rows = slice(at, at + STEP)
-                terms = []
-                for j in range(2):
+                for m in halves:
+                    for c in halves:
+                        rows = slice(m * HALF + rr, m * HALF + rr + STEP)
+                        a, b = undone[e, 0, rows, lanes(0, c)], undone[e, 1, rows, lanes(0, c)]
+                        rows = slice(c * HALF + rr, c * HALF + rr + STEP)
+                        back[e, rows, lanes(m * N, 0)] = (a + b).astype(bf16)
+                        back[e, rows, lanes(m * N, 1)] = (a - b).astype(bf16)
+        for e in halves:
+            chi[e] = jnp.dot(tab[2 + e], back[e], preferred_element_type=f32)
+        for rr in range(0, HALF, STEP):
+            terms = [[None, None], [None, None]]
+            for j in halves:
+                waves = []
+                for m in halves:
+                    parts = [
+                        [chi[e, c * HALF + rr : c * HALF + rr + STEP, lanes(m * N, j)] for e in halves]
+                        for c in halves
+                    ]
+                    waves.append([(a + b, a - b) for a, b in parts])
+                for e in halves:
+                    at = e * HALF + rr
+                    rows = slice(at, at + STEP)
                     o_re, o_im = patch[p, 0, j, rows, :], patch[p, 1, j, rows, :]
                     g_re = g_im = 0.0
-                    for m in range(2):
-                        p_re = pr[2 * m, rows, j * LANES : (j + 1) * LANES]
-                        p_im = pr[2 * m + 1, rows, j * LANES : (j + 1) * LANES]
-                        cols = slice(m * N + j * LANES, m * N + (j + 1) * LANES)
-                        b_re = chi[rb, rr : rr + STEP, cols]
-                        b_im = chi[rb, HALF + rr : HALF + rr + STEP, cols]
+                    for m in halves:
+                        p_re, p_im = pr[2 * m, rows, lanes(0, j)], pr[2 * m + 1, rows, lanes(0, j)]
+                        b_re, b_im = waves[m][0][e], waves[m][1][e]
                         g_re += p_re * b_re + p_im * b_im
                         g_im += p_re * b_im - p_im * b_re
                         h_re = o_re * b_re + o_im * b_im
@@ -306,11 +331,12 @@
                         pair = (b // (nx * ny), b // ny % nx, slice(b % ny, b % ny + 2))
                         part[it][(*pair, 4 * m + j)] += h_re.reshape(2, 8, LANES)
                         part[it][(*pair, 4 * m + 2 + j)] += h_im.reshape(2, 8, LANES)
-                    terms.append((g_re, g_im))
-                put = slice(FAR + at, FAR + at + STEP)
+                    terms[e][j] = g_re, g_im
+            for e in halves:
+                put = slice(FAR + e * HALF + rr, FAR + e * HALF + rr + STEP)
                 for ch in range(2):
-                    a = pltpu.roll(terms[0][ch], ahead, 1)
-                    b = pltpu.roll(terms[1][ch], ahead, 1)
+                    a = pltpu.roll(terms[e][0][ch], ahead, 1)
+                    b = pltpu.roll(terms[e][1][ch], ahead, 1)
                     placed[p, 0, ch, put, :] = jnp.where(late, a, 0.0)
                     placed[p, 1, ch, put, :] = jnp.where(late, b, a)
                     placed[p, 2, ch, put, :] = jnp.where(late, 0.0, b)
@@ -358,6 +384,7 @@
 
     for load in loads:
         load.wait()
+    lax.fori_loop(0, SLOTS, order_amplitudes, 0)
     rows_w = illuminate(0)
     waiting = spread(field[0], sent_up, sent_down, sent_middle, forwards)
     arrive(waiting)
@@ -437,6 +464,15 @@
             at = ys[order[n]]
             hs[it][:, at] = part[it][core, :, at] + rc[it][:, at]
 
+        def send_sides(lo, hi, it=it):
+            return [
+                send(own[it].at[0, :, lo:hi, :], from_right[it].at[:, lo:hi, :], left),
+                send(own[it].at[2, :, lo:hi, :], from_left[it].at[:, lo:hi, :], right),
+            ]
+
+        total(grads, own[it], LANES, *MIDDLE)
+        side_middle = send_sides(*MIDDLE)
+
         sum_core(0)
         far = [
             [
@@ -445,15 +481,6 @@
             ]
             for h, p in enumerate(planes)
         ]
-
-        def send_sides(lo, hi, it=it):
-            return [
-                send(own[it].at[0, :, lo:hi, :], from_right[it].at[:, lo:hi, :], left),
-                send(own[it].at[2, :, lo:hi, :], from_left[it].at[:, lo:hi, :], right),
-            ]
-
-        total(grads, own[it], LANES, *MIDDLE)
-        side_middle = send_sides(*MIDDLE)
 
         sum_core(1)
         sum_core(2)
@@ -606,7 +633,7 @@
     nz = nd // 4
     nx = nd // nz
     blocks = 2 * nx * ny
-    args = tables()
+    table = tables()
 
     def vmem(*shape, dtype=jnp.float32):
         return pltpu.VMEM(shape, dtype)
@@ -617,7 +644,6 @@
     def local(sample, probe, amps, rows_at, cols_at, live):
         hbm = pl.BlockSpec(memory_space=pl.ANY)
         smem = pl.BlockSpec(memory_space=pltpu.SMEM)
-        square = (2 * N, 2 * N)
         f32 = jnp.float32
         raw_sample, raw_probe, sums, weight = pl.pallas_call(
             functools.partial(kernel, (nx, ny, nz)),
@@ -627,17 +653,19 @@
                 jax.ShapeDtypeStruct((2, nx, ny, 8, 8, LANES), f32),
                 jax.ShapeDtypeStruct((blocks, 2, 8, LANES), f32),
             ],
-            in_specs=[hbm] * 7 + [smem] * 3,
+            in_specs=[hbm] * 4 + [smem] * 3,
             out_specs=[hbm] * 4,
             scratch_shapes=[
                 *two(3, 2, EXT, LANES),
                 *two(4, N, N),
                 vmem(SLOTS, N, N),
-                *[vmem(*square, dtype=jnp.bfloat16)] * 4,
+                vmem(6, N, N, dtype=jnp.bfloat16),
                 vmem(SLOTS, 2, 2, N, LANES),
-                *[vmem(*square, dtype=jnp.bfloat16)] * 2,
-                *[vmem(2, 2 * HALF, 2 * N, dtype=jnp.bfloat16)] * 2,
-                *[vmem(2, 2 * HALF, 2 * N)] * 2,
+                *[vmem(2, N, 2 * N, dtype=jnp.bfloat16)] * 2,
+                *[vmem(2, 2, N, N, dtype=jnp.bfloat16)] * 2,
+                vmem(2, N, 2 * N),
+                *[vmem(2, 2, N, N)] * 2,
+                vmem(2, N, 2 * N),
                 vmem(2, N, LANES),
                 vmem(SLOTS, 3, 2, 2 * FAR + N, LANES),
                 *two(3, 2, LANES, LANES),
@@ -673,7 +701,7 @@
                 *two(ny - 1, 2, 8, LANES),
                 *two(nz, 2, 8, LANES),
                 *two(blocks, 2, 8, LANES),
-                pltpu.SemaphoreType.DMA((13,)),
+                pltpu.SemaphoreType.DMA((10,)),
                 pltpu.SemaphoreType.DMA((COPIES,)),
                 pltpu.SemaphoreType.DMA((COPIES,)),
             ],
@@ -683,7 +711,7 @@
             cost_estimate=pl.CostEstimate(
                 flops=2 * 4 * 4 * 2 * 512**3, bytes_accessed=6 << 20, transcendentals=8 * N * N
             ),
-        )(sample, probe.reshape(4, N, N), amps, *args, rows_at, cols_at, live)
+        )(sample, probe.reshape(4, N, N), amps, table, rows_at, cols_at, live)
         steps = 4
         some, rows = blocks // steps, N // steps
         tile = pl.BlockSpec((2, BAND // steps, LANES), lambda i: (0, i, 0))

time: 150 us -> 149 us (level)
  Pallas kernels: 149 us -> 147 us
where the time goes in v4:
time: 149 us
  Pallas kernels  147 us (99%)
    pallas_call x1, Pallas kernels, local(): pl.pallas_call(functools.partial(kernel, (nx, ny, nz)), out_shape=[jax.Sh...  143 us
    pallas_call x1, Pallas kernels, local(): pl.pallas_call(functools.partial(finish, 1.0 / math.sqrt(SLOTS * ng * nd)...  4.01 us

profile of v4, /device:TPU:1, one launch (start us, length us, event | category | flops | bytes accessed | tf_op | source)
XLA Modules:
  0.0 148.7 jit_solution(12753527833515128787)
XLA Ops:
  1.3 143.4 %shard_map.94 = (f32[2,512,128]{2,1,0:T(8,128)}, f32[4,256,256]{2,1,0:T(8,128)}, f32[2,4,4,8,8,128]{5,4,3,2,1,0:T(8,128)}, f32[32,2,8,128]{3,2,1,0:T(8,128)}) custom-call(f32[2,512,128]{2,1,0:T(8,128)} %refs_0_.1, f32[4,256,256]{2,1,0:T(8,128)} %bitcast.3, f32[4,256,256]{2,1,0:T(8,128)} %refs_2_.1, bf16[6,256,256]{2,1,0:T(8,128)(2,1)} %constant.2.clone.refs_3_, ...), custom_call_target="tpu_custom_call" | custom-call | flops 8589934592 | bytes 6291456 | tf_op jit(solution)/shard_map/pallas_call | solution.py:648
  144.7 4.0 %shard_map.95 = (f32[2,512,128]{2,1,0:T(8,128)}, f32[2,2,256,256]{3,2,1,0:T(8,128)}, f32[2,2,256,256]{3,2,1,0:T(8,128)}) custom-call(f32[2,512,128]{2,1,0:T(8,128)} %get-tuple-element.7.sample, f32[4,256,256]{2,1,0:T(8,128)} %get-tuple-element.8.probe, f32[32,8,8,128]{3,2,1,0:T(8,128)} %bitcast.2, f32[32,2,8,128]{3,2,1,0:T(8,128)} %get-tuple-element.10.weight), custom_call_target="tpu_custom_call" | custom-call | flops 1048576 | bytes 6291456 | tf_op jit(solution)/shard_map/pallas_call | solution.py:719

commit v5 on v4

--- a/solution.py
+++ b/solution.py
@@ -38,8 +38,8 @@
 
 def kernel(shape, *refs):
     sample, probe, amps, table, rows_at, cols_at, live = refs[:7]
-    out_sample, out_probe, out_sums, out_weight = refs[7:11]
-    scratch = iter(refs[11:])
+    out_sample, out_probe, out_sums = refs[7:10]
+    scratch = iter(refs[10:])
 
     def two():
         return next(scratch), next(scratch)
@@ -50,9 +50,8 @@
         next(scratch) for _ in range(13)
     )
     halo_up, halo_dn, own, from_up, from_dn, from_left, from_right = (two() for _ in range(7))
-    w_up, w_dn, w_own, w_from_up, w_from_dn, w_left, w_right = (two() for _ in range(7))
-    part, rc, hs, r1, r2, hy, rx, zb, rz, zg, full = (two() for _ in range(11))
-    vpart, vrc, vhs, vrx, vhx, vry, vz, vfull = (two() for _ in range(8))
+    w_all, w_left, w_right, w_from_up, w_from_dn = (two() for _ in range(5))
+    part, rc, hs, rxy, zb, rz, rv, zg, full = (two() for _ in range(9))
     load_sem, send_sem, recv_sem = scratch
 
     g, d = lax.axis_index("grp"), lax.axis_index("dev")
@@ -67,8 +66,7 @@
     xs = [(x + k) % nx for k in range(nx)]
     ys = [(y + k) % ny for k in range(ny)]
     zs = [(z + k) % nz for k in range(nz)]
-    on_x = [{"grp": g, "dev": v * nz + z} for v in xs]
-    on_y = [{"grp": v * 2 + core, "dev": d} for v in ys]
+    on_xy = [[{"grp": v * 2 + core, "dev": u * nz + z} for v in ys] for u in xs]
     on_z = [{"grp": g, "dev": x * nz + v} for v in zs]
 
     copies = []
@@ -100,7 +98,8 @@
         load.start()
 
     barrier = pltpu.get_barrier_semaphore()
-    peers = [above, below, left, right, partner] + on_x[1:] + on_y[1:] + on_z[1:]
+    peers = [above, below, left, right, partner] + on_z[1:]
+    peers += [on_xy[i][j] for i in range(nx) for j in range(ny) if i or j]
     for peer in peers:
         pl.semaphore_signal(barrier, inc=1, device_id=peer, device_id_type=MESH)
     pl.semaphore_wait(barrier, len(peers))
@@ -155,7 +154,6 @@
     lax.fori_loop(0, FAR // STEP, clear, 0)
     for it in range(2):
         part[it][...] = jnp.zeros(part[it].shape, jnp.float32)
-        vpart[it][...] = jnp.zeros(vpart[it].shape, jnp.float32)
 
     def placing(p):
         s = jnp.clip(cols_at[p] - col_anchor, 0, LANES)
@@ -200,12 +198,11 @@
             return 0
 
         lax.fori_loop(0, SLOTS, place, 0)
-        total(lights, w_up[it], 0, 0, LANES)
-        up = send(w_up[it], w_from_dn[it], above)
-        total(lights, w_dn[it], LANES + BAND, 0, LANES)
-        down = send(w_dn[it], w_from_up[it], below)
-        total(lights, w_own[it], LANES, 0, BAND)
-        return [up, down]
+        total(lights, w_all[it], 0, 0, EXT)
+
+    def pair_at(row):
+        b = row // 8
+        return b // (nx * ny), b // ny % nx, slice(b % ny, b % ny + 2)
 
     def gather(it):
         f = field[it]
@@ -227,7 +224,7 @@
                     patch[p, 0, j, rows, :] = o_re
                     patch[p, 1, j, rows, :] = o_im
                     v = jnp.where(used, o_re * o_re + o_im * o_im, 0.0).reshape(2, 8, LANES)
-                    vpart[it][rr // 8 : rr // 8 + 2, j] += v
+                    part[it][(*pair_at(rr), 8 + j)] += v
             return 0
 
         lax.fori_loop(0, SLOTS, body, 0)
@@ -327,8 +324,7 @@
                         g_im += p_re * b_im - p_im * b_re
                         h_re = o_re * b_re + o_im * b_im
                         h_im = o_re * b_im - o_im * b_re
-                        b = at // 8
-                        pair = (b // (nx * ny), b // ny % nx, slice(b % ny, b % ny + 2))
+                        pair = pair_at(at)
                         part[it][(*pair, 4 * m + j)] += h_re.reshape(2, 8, LANES)
                         part[it][(*pair, 4 * m + 2 + j)] += h_im.reshape(2, 8, LANES)
                     terms[e][j] = g_re, g_im
@@ -344,7 +340,7 @@
     def update(it, lo, hi):
         for rr in range(lo, hi, 2 * STEP):
             rows = slice(rr, rr + 2 * STEP)
-            scale = w_own[it][1, rows, :]
+            scale = w_all[it][1, LANES + rr : LANES + rr + 2 * STEP, :]
             for ch in range(2):
                 grad = own[it][1, ch, rows, :] + (from_left[it][ch, rows, :] + from_right[it][ch, rows, :])
                 value = field[it][1, ch, LANES + rr : LANES + rr + 2 * STEP, :] + grad * scale
@@ -362,7 +358,7 @@
             c, xy = i // (nx * ny), i % (nx * ny)
             for j in range(2):
                 cols = slice(j * LANES, (j + 1) * LANES)
-                scale = 1.0 / (vfull[0][i, j] + PROBE_DAMPING)
+                scale = 1.0 / (full[0][c, xy // ny, xy % ny, 8 + j] + PROBE_DAMPING)
                 for q in range(4):
                     grad = full[0][c, xy // ny, xy % ny, 2 * q + j]
                     prb[1][q, at, cols] = prb[0][q, at, cols] + grad * scale
@@ -385,7 +381,7 @@
     for load in loads:
         load.wait()
     lax.fori_loop(0, SLOTS, order_amplitudes, 0)
-    rows_w = illuminate(0)
+    illuminate(0)
     waiting = spread(field[0], sent_up, sent_down, sent_middle, forwards)
     arrive(waiting)
 
@@ -395,74 +391,21 @@
             gather(0)
         else:
             write(prb[1], out_probe)
-            rows_w = illuminate(1)
-
-        mine = vfull[it].at[(core * nx + x) * ny + y]
-        v_core = remote(vpart[it].at[pl.ds((1 - core) * half, half)], vrc[it], partner)
-        v_x = [remote(vhs[it].at[pl.ds(xs[k] * ny, ny)], vrx[it].at[k - 1], on_x[k]) for k in range(1, nx)]
-        v_y = [remote(vhx[it].at[ys[k]], vry[it].at[k - 1], on_y[k]) for k in range(1, ny)]
-        v_z = [remote(vz[it].at[z], vz[it].at[z], on_z[k]) for k in range(1, nz)]
-        v_back_y = [remote(mine, mine, on_y[k]) for k in range(1, ny)]
-        row = vfull[it].at[pl.ds((core * nx + x) * ny, ny)]
-        v_back_x = [remote(row, row, on_x[k]) for k in range(1, nx)]
-        whole = vfull[it].at[pl.ds(core * half, half)]
-        v_back_core = remote(whole, whole, partner)
-        w_sides = [
-            remote(w_own[it].at[0], w_right[it], left),
-            remote(w_own[it].at[2], w_left[it], right),
+            illuminate(1)
+
+        sides_w = [
+            send(w_all[it].at[0], w_right[it], left),
+            send(w_all[it].at[2], w_left[it], right),
         ]
-        v_core.start()
-
-        def weight_core(it=it, v_core=v_core, v_x=v_x):
-            v_core.wait_recv()
-            vhs[it][...] = vpart[it][pl.ds(core * half, half)] + vrc[it][...]
-            start(v_x)
-
-        def weight_x(it=it, v_x=v_x, v_y=v_y):
-            arrive(v_x)
-            value = vhs[it][pl.ds(x * ny, ny)]
-            for k in range(nx - 1):
-                value += vrx[it][k]
-            vhx[it][...] = value
-            start(v_y)
-
-        def light_sides(it=it, rows_w=rows_w, w_sides=w_sides):
-            arrive(rows_w)
-            for t in range(3):
-                w_own[it][t, 0:LANES, :] += w_from_up[it][t]
-                w_own[it][t, BAND - LANES : BAND, :] += w_from_dn[it][t]
-            start(w_sides)
-
-        def weight_y(it=it, v_y=v_y, v_z=v_z):
-            arrive(v_y)
-            value = vhx[it][y]
-            for k in range(ny - 1):
-                value += vry[it][k]
-            vz[it][z] = value
-            start(v_z)
-
-        def visit(p, _, it=it, hooks=(weight_core, weight_x, light_sides, weight_y)):
-            for n, hook in zip((1, 2, 2, 3), hooks, strict=True):
-                pl.when(p == n)(hook)
-            position(it, p)
-            return 0
-
-        lax.fori_loop(0, SLOTS, visit, 0)
-
-        sums, mates = part[it], rc[it]
+        lax.fori_loop(0, SLOTS, lambda p, _, it=it: (position(it, p), 0)[1], 0)
+
         order = (2, 1, 3, 0)
-        swap = [send(sums.at[1 - core, :, ys[k]], mates.at[:, ys[k]], partner) for k in order]
-        planes = [slice(4 * h, 4 * h + 4) for h in range(2)]
+        swap = [send(part[it].at[1 - core, xs[i]], rc[it].at[xs[i]], partner) for i in order]
 
         total(grads, halo_up[it], 0, 0, LANES)
         rows_up = send(halo_up[it], from_dn[it], above)
         total(grads, halo_dn[it], LANES + BAND, 0, LANES)
         rows_down = send(halo_dn[it], from_up[it], below)
-
-        def sum_core(n, it=it, swap=swap):
-            swap[n].wait_recv()
-            at = ys[order[n]]
-            hs[it][:, at] = part[it][core, :, at] + rc[it][:, at]
 
         def send_sides(lo, hi, it=it):
             return [
@@ -473,32 +416,24 @@
         total(grads, own[it], LANES, *MIDDLE)
         side_middle = send_sides(*MIDDLE)
 
-        sum_core(0)
-        far = [
-            [
-                send(hs[it].at[0:2, ys[2], p], r1[it].at[0, h], on_y[1]),
-                send(hs[it].at[2:4, ys[2], p], r1[it].at[1, h], on_y[3]),
-            ]
-            for h, p in enumerate(planes)
-        ]
-
-        sum_core(1)
-        sum_core(2)
-        near = []
-        for h, p in enumerate(planes):
-            arrive(far[h])
-            hs[it][0:2, ys[1], p] += r1[it][0, h]
-            hs[it][2:4, ys[3], p] += r1[it][1, h]
-            near.append(
-                [
-                    send(hs[it].at[:, ys[1], p], r2[it].at[0, h], on_y[1]),
-                    send(hs[it].at[:, ys[3], p], r2[it].at[1, h], on_y[3]),
-                ]
-            )
-        sum_core(3)
+        to_plane = []
+        for n, i in enumerate(order):
+            swap[n].wait_recv()
+            at = xs[i]
+            hs[it][at] = part[it][core, at] + rc[it][at]
+            for j in (2, 1, 3, 0):
+                if i or j:
+                    to_plane.append(send(hs[it].at[at, ys[j]], rxy[it].at[i * ny + j - 1], on_xy[i][j]))
 
         total(grads, own[it], LANES, *UP)
         total(grads, own[it], LANES, *DOWN)
+
+        arrive(sides_w)
+        w_all[it][1] += w_left[it][...] + w_right[it][...]
+        rows_w = [
+            send(w_all[it].at[1, 0:LANES, :], w_from_dn[it], above),
+            send(w_all[it].at[1, LANES + BAND : EXT, :], w_from_up[it], below),
+        ]
 
         def add_rows(src, lo, it=it):
             for t in range(3):
@@ -512,33 +447,19 @@
         add_rows(from_dn[it], DOWN[0])
         side_down = send_sides(*DOWN)
 
-        to_x = []
-        for h, p in enumerate(planes):
-            arrive(near[h])
-            hy[it][h] = hs[it][:, y, p] + (r2[it][0, h] + r2[it][1, h])
-            to_x.append([send(hy[it].at[h, xs[k]], rx[it].at[h, k - 1], on_x[k]) for k in range(1, nx)])
-
-        arrive(v_z)
-        value = vz[it][0]
-        for k in range(1, nz):
-            value += vz[it][k]
-        vfull[it][(core * nx + x) * ny + y] = value
-        start(v_back_y)
-
-        arrive(w_sides)
-        lit = w_own[it][1] + (w_left[it][...] + w_right[it][...])
-        w_own[it][1] = 1.0 / (lit + SAMPLE_DAMPING)
-
-        for h, p in enumerate(planes):
-            arrive(to_x[h])
-            value = hy[it][h, x]
-            for k in range(nx - 1):
-                value += rx[it][h, k]
-            zb[it][p] = value
+        arrive(to_plane)
+        value = hs[it][x, y]
+        for k in range(nx * ny - 1):
+            value += rxy[it][k]
+        zb[it][0:8] = value[0:8]
+        rv[it][z] = value[8:10]
         to_z = [send(zb[it].at[zs[k]], rz[it].at[k - 1], on_z[k]) for k in range(1, nz)]
-
-        arrive(v_back_y)
-        start(v_back_x)
+        to_z += [send(rv[it].at[z], rv[it].at[z], on_z[k]) for k in range(1, nz)]
+
+        arrive(rows_w)
+        w_all[it][1, LANES : 2 * LANES, :] += w_from_up[it][...]
+        w_all[it][1, BAND : LANES + BAND, :] += w_from_dn[it][...]
+        w_all[it][1, LANES : LANES + BAND, :] = 1.0 / (w_all[it][1, LANES : LANES + BAND, :] + SAMPLE_DAMPING)
 
         arrive(side_middle)
         update(it, *MIDDLE)
@@ -549,6 +470,11 @@
             value += rz[it][k]
         zg[it][z] = value
         back_z = [send(zg[it].at[z], zg[it].at[z], on_z[k]) for k in range(1, nz)]
+        result = full[it]
+        value = rv[it][0]
+        for k in range(1, nz):
+            value += rv[it][k]
+        result[core, x, y, 8:10] = value
 
         arrive(side_up)
         update(it, *UP)
@@ -561,14 +487,9 @@
             forwards = [forward_up(field[1], 1)]
 
         arrive(back_z)
-        result = full[it]
-        result[core, x, y] = zg[it][...]
-        mine = [result.at[core, x, y, p] for p in planes]
-        back_x = [[send(m, m, on_x[k]) for k in range(1, nx)] for m in mine]
-        arrive(v_back_x)
-        v_back_core.start()
-        if it == 1:
-            flush()
+        result[core, x, y, 0:8] = zg[it][...]
+        mine = result.at[core, x, y]
+        returned = {(i, j): send(mine, mine, on_xy[i][j]) for i in order for j in order if i or j}
 
         arrive(side_down)
         update(it, *DOWN)
@@ -576,36 +497,20 @@
             sent_down = send_columns(field[1], updated, *DOWN)
             forwards.append(forward_down(field[1], 1))
             sent_middle = send_columns(field[1], updated, *MIDDLE)
-
-        def to_core(k, result=result):
-            piece = result.at[core, :, ys[k]]
-            return send(piece, piece, partner)
-
-        back_near = []
-        for h, p in enumerate(planes):
-            arrive(back_x[h])
-            mine = result.at[core, :, y, p]
-            back_near.append([send(mine, mine, on_y[k]) for k in (1, 3)])
-        back_core = [to_core(0)]
-        back_far = []
-        for h, p in enumerate(planes):
-            arrive(back_near[h])
-            low, high = result.at[core, 0:2, ys[3], p], result.at[core, 2:4, ys[1], p]
-            back_far.append([send(low, low, on_y[1]), send(high, high, on_y[3])])
-        back_core += [to_core(1), to_core(3)]
+        else:
+            flush()
+
+        back_core = []
+        for i in (0, 1, 3, 2):
+            arrive([returned[i, j] for j in range(ny) if i or j])
+            piece = result.at[core, xs[(nx - i) % nx]]
+            back_core.append(send(piece, piece, partner))
         if it == 0:
-            waiting = spread(field[1], sent_up, sent_down, sent_middle, forwards)
-        for h in range(2):
-            arrive(back_far[h])
-        back_core.append(to_core(2))
-        v_back_core.wait_recv()
-        if it == 0:
-            arrive(waiting)
+            arrive(spread(field[1], sent_up, sent_down, sent_middle, forwards))
             gather(1)
             arrive(back_core)
             finish_probe()
         else:
-            write(vfull[1], out_weight)
             flush()
             arrive(back_core)
             write(full[1], out_sums)
@@ -614,13 +519,13 @@
         copy.wait()
 
 
-def finish(scale, sample, probe, sums, weight, new_sample, new_probe, probe_gradient):
+def finish(scale, sample, probe, sums, new_sample, new_probe, probe_gradient):
     new_sample[...] = sample[...]
     for b in range(sums.shape[0]):
         rows = slice(8 * b, 8 * b + 8)
         for j in range(2):
             cols = slice(j * LANES, (j + 1) * LANES)
-            damped = 1.0 / (weight[b, j] + PROBE_DAMPING)
+            damped = 1.0 / (sums[b, 8 + j] + PROBE_DAMPING)
             for q in range(4):
                 grad = sums[b, 2 * q + j]
                 new_probe[q // 2, q % 2, rows, cols] = probe[q, rows, cols] + grad * damped
@@ -645,16 +550,15 @@
         hbm = pl.BlockSpec(memory_space=pl.ANY)
         smem = pl.BlockSpec(memory_space=pltpu.SMEM)
         f32 = jnp.float32
-        raw_sample, raw_probe, sums, weight = pl.pallas_call(
+        raw_sample, raw_probe, sums = pl.pallas_call(
             functools.partial(kernel, (nx, ny, nz)),
             out_shape=[
                 jax.ShapeDtypeStruct((2, BAND, LANES), f32),
                 jax.ShapeDtypeStruct((4, N, N), f32),
-                jax.ShapeDtypeStruct((2, nx, ny, 8, 8, LANES), f32),
-                jax.ShapeDtypeStruct((blocks, 2, 8, LANES), f32),
+                jax.ShapeDtypeStruct((2, nx, ny, 10, 8, LANES), f32),
             ],
             in_specs=[hbm] * 4 + [smem] * 3,
-            out_specs=[hbm] * 4,
+            out_specs=[hbm] * 3,
             scratch_shapes=[
                 *two(3, 2, EXT, LANES),
                 *two(4, N, N),
@@ -675,33 +579,21 @@
                 *two(3, 2, LANES, LANES),
                 *two(2, BAND, LANES),
                 *two(2, BAND, LANES),
-                *two(3, LANES, LANES),
-                *two(3, LANES, LANES),
-                *two(3, BAND, LANES),
-                *two(3, LANES, LANES),
-                *two(3, LANES, LANES),
-                *two(BAND, LANES),
-                *two(BAND, LANES),
-                *two(2, nx, ny, 8, 8, LANES),
-                *two(nx, ny, 8, 8, LANES),
-                *two(nx, ny, 8, 8, LANES),
-                *two(2, 2, nx // 2, 4, 8, LANES),
-                *two(2, 2, nx, 4, 8, LANES),
-                *two(2, nx, 4, 8, LANES),
-                *two(2, nx - 1, 4, 8, LANES),
+                *two(3, EXT, LANES),
+                *two(EXT, LANES),
+                *two(EXT, LANES),
+                *two(LANES, LANES),
+                *two(LANES, LANES),
+                *two(2, nx, ny, 10, 8, LANES),
+                *two(nx, ny, 10, 8, LANES),
+                *two(nx, ny, 10, 8, LANES),
+                *two(nx * ny - 1, 10, 8, LANES),
                 *two(8, 8, LANES),
                 *two(nz - 1, 8, LANES),
+                *two(nz, 2, 8, LANES),
                 *two(8, 8, LANES),
-                *two(2, nx, ny, 8, 8, LANES),
-                *two(blocks, 2, 8, LANES),
-                *two(blocks // 2, 2, 8, LANES),
-                *two(blocks // 2, 2, 8, LANES),
-                *two(nx - 1, ny, 2, 8, LANES),
-                *two(ny, 2, 8, LANES),
-                *two(ny - 1, 2, 8, LANES),
-                *two(nz, 2, 8, LANES),
-                *two(blocks, 2, 8, LANES),
-                pltpu.SemaphoreType.DMA((10,)),
+                *two(2, nx, ny, 10, 8, LANES),
+                pltpu.SemaphoreType.DMA((9,)),
                 pltpu.SemaphoreType.DMA((COPIES,)),
                 pltpu.SemaphoreType.DMA((COPIES,)),
             ],
@@ -727,13 +619,12 @@
             in_specs=[
                 tile,
                 pl.BlockSpec((4, rows, N), lambda i: (0, i, 0)),
-                pl.BlockSpec((some, 8, 8, LANES), lambda i: (i, 0, 0, 0)),
-                pl.BlockSpec((some, 2, 8, LANES), lambda i: (i, 0, 0, 0)),
+                pl.BlockSpec((some, 10, 8, LANES), lambda i: (i, 0, 0, 0)),
             ],
             out_specs=[tile, modes, modes],
             compiler_params=pltpu.CompilerParams(vmem_limit_bytes=60 * 1024 * 1024),
             cost_estimate=pl.CostEstimate(flops=16 * N * N, bytes_accessed=6 << 20, transcendentals=0),
-        )(raw_sample, raw_probe, sums.reshape(blocks, 8, 8, LANES), weight)
+        )(raw_sample, raw_probe, sums.reshape(blocks, 10, 8, LANES))
 
     return jax.shard_map(
         local,

time: 149 us -> 149 us (level)
  no operation moved by 1% of the time
where the time goes in v5:
time: 149 us
  Pallas kernels  147 us (99%)
    pallas_call x1, Pallas kernels, local(): pl.pallas_call(functools.partial(kernel, (nx, ny, nz)), out_shape=[jax.Sh...  143 us
    pallas_call x1, Pallas kernels, local(): pl.pallas_call(functools.partial(finish, 1.0 / math.sqrt(SLOTS * ng * nd)...  4.05 us

profile of v5, /device:TPU:1, one launch (start us, length us, event | category | flops | bytes accessed | tf_op | source)
XLA Modules:
  0.0 148.7 jit_solution(2227144530102022052)
XLA Ops:
  1.3 143.4 %shard_map.94 = (f32[2,512,128]{2,1,0:T(8,128)}, f32[4,256,256]{2,1,0:T(8,128)}, f32[2,4,4,10,8,128]{5,4,3,2,1,0:T(8,128)}) custom-call(f32[2,512,128]{2,1,0:T(8,128)} %refs_0_.1, f32[4,256,256]{2,1,0:T(8,128)} %bitcast.3, f32[4,256,256]{2,1,0:T(8,128)} %refs_2_.1, bf16[6,256,256]{2,1,0:T(8,128)(2,1)} %constant.2.clone.refs_3_, s32[4]{0:T(128)} %refs_4_.1, ...), custom_call_target="tpu_custom_call" | custom-call | flops 8589934592 | bytes 6291456 | tf_op jit(solution)/shard_map/pallas_call | solution.py:553
  144.7 4.1 %shard_map.95 = (f32[2,512,128]{2,1,0:T(8,128)}, f32[2,2,256,256]{3,2,1,0:T(8,128)}, f32[2,2,256,256]{3,2,1,0:T(8,128)}) custom-call(f32[2,512,128]{2,1,0:T(8,128)} %get-tuple-element.6.sample, f32[4,256,256]{2,1,0:T(8,128)} %get-tuple-element.7.probe, f32[32,10,8,128]{3,2,1,0:T(8,128)} %bitcast.2), custom_call_target="tpu_custom_call" | custom-call | flops 1048576 | bytes 6291456 | tf_op jit(solution)/shard_map/pallas_call | solution.py:611

commit v6 on v4

--- a/solution.py
+++ b/solution.py
@@ -50,7 +50,8 @@
         next(scratch) for _ in range(13)
     )
     halo_up, halo_dn, own, from_up, from_dn, from_left, from_right = (two() for _ in range(7))
-    w_up, w_dn, w_own, w_from_up, w_from_dn, w_left, w_right = (two() for _ in range(7))
+    told, heard, known = (next(scratch) for _ in range(3))
+    w_own, w_from_up, w_from_dn = (two() for _ in range(3))
     part, rc, hs, r1, r2, hy, rx, zb, rz, zg, full = (two() for _ in range(11))
     vpart, vrc, vhs, vrx, vhx, vry, vz, vfull = (two() for _ in range(8))
     load_sem, send_sem, recv_sem = scratch
@@ -109,8 +110,17 @@
     col_anchor = d * LANES - LANES
     starts = [jnp.clip(rows_at[p] - row_anchor, 0, FAR) for p in range(SLOTS)]
 
-    def alive(p):
-        return jnp.full((STEP, LANES), p, jnp.int32) < jnp.full((STEP, LANES), live[0], jnp.int32)
+    shifts = [jnp.clip(cols_at[p] - col_anchor, 0, LANES) for p in range(SLOTS)]
+
+    def alive(p, count):
+        return jnp.full((STEP, LANES), p, jnp.int32) < jnp.full((STEP, LANES), count, jnp.int32)
+
+    place_in_row = lax.broadcasted_iota(jnp.int32, (8, LANES), 1)
+    facts = jnp.zeros((8, LANES), jnp.int32)
+    for n, fact in enumerate([*starts, *shifts, live[0]]):
+        facts = jnp.where(place_in_row == n, fact, facts)
+    told[...] = facts
+    tell = [send(told, heard.at[0], right), send(told, heard.at[1], left)]
 
     def send_columns(f, source, lo, hi):
         src = source(lo, hi)
@@ -178,7 +188,6 @@
         lax.fori_loop(0, (hi - lo) // (2 * STEP), body, 0)
 
     grads = [((t, ch), (t, ch)) for t in range(3) for ch in range(2)]
-    lights = [((t, 0), (t,)) for t in range(3)]
 
     def illuminate(it):
         for j in range(2):
@@ -186,26 +195,40 @@
             value = prb[it][0, :, cols] ** 2 + prb[it][1, :, cols] ** 2
             light[j] = value + (prb[it][2, :, cols] ** 2 + prb[it][3, :, cols] ** 2)
 
+        zero = jnp.zeros((STEP, LANES), jnp.float32)
+        lane = lax.broadcasted_iota(jnp.int32, (STEP, LANES), 1)
+
         def place(p, _):
-            ahead, late = placing(p)
-            used = alive(p)
-            for rr in range(0, N, STEP):
-                a, b = (
-                    pltpu.roll(jnp.where(used, light[j, rr : rr + STEP, :], 0.0), ahead, 1) for j in range(2)
-                )
-                at = slice(FAR + rr, FAR + rr + STEP)
-                placed[p, 0, 0, at, :] = jnp.where(late, a, 0.0)
-                placed[p, 1, 0, at, :] = jnp.where(late, b, a)
-                placed[p, 2, 0, at, :] = jnp.where(late, 0.0, b)
+            for t in range(3):
+                shift = known[t, 0, SLOTS + p]
+                late = lane >= shift
+                used = alive(p, known[t, 0, 2 * SLOTS])
+                for rr in range(0, N, STEP):
+                    a, b = (
+                        pltpu.roll(jnp.where(used, light[j, rr : rr + STEP, :], 0.0), shift % LANES, 1)
+                        for j in range(2)
+                    )
+                    value = (jnp.where(late, zero, b), jnp.where(late, b, a), jnp.where(late, a, zero))[t]
+                    placed[p, t, 0, FAR + rr : FAR + rr + STEP, :] = value
             return 0
 
         lax.fori_loop(0, SLOTS, place, 0)
-        total(lights, w_up[it], 0, 0, LANES)
-        up = send(w_up[it], w_from_dn[it], above)
-        total(lights, w_dn[it], LANES + BAND, 0, LANES)
-        down = send(w_dn[it], w_from_up[it], below)
-        total(lights, w_own[it], LANES, 0, BAND)
-        return [up, down]
+
+        def body(i, _):
+            rr = pl.multiple_of(i * 2 * STEP, 2 * STEP)
+            values = [
+                placed[p, t, 0, pl.ds(FAR + rr - known[t, 0, p], 2 * STEP), :]
+                for t in range(3)
+                for p in range(SLOTS)
+            ]
+            w_own[it][pl.ds(rr, 2 * STEP), :] = sum(values[1:], values[0])
+            return 0
+
+        lax.fori_loop(0, EXT // (2 * STEP), body, 0)
+        return [
+            send(w_own[it].at[0:LANES, :], w_from_dn[it], above),
+            send(w_own[it].at[LANES + BAND : EXT, :], w_from_up[it], below),
+        ]
 
     def gather(it):
         f = field[it]
@@ -215,7 +238,7 @@
             s = jnp.clip(cols_at[p] - col_anchor, 0, LANES)
             behind = (LANES - s) % LANES
             early = lax.broadcasted_iota(jnp.int32, (STEP, LANES), 1) < LANES - s
-            used = alive(p)
+            used = alive(p, live[0])
             for rr in range(0, N, STEP):
                 rows = slice(rr, rr + STEP)
                 halves = []
@@ -247,7 +270,7 @@
     def position(it, p):
         pr = prb[it]
         ahead, late = placing(p)
-        used = alive(p)
+        used = alive(p, live[0])
         f32, bf16 = jnp.float32, jnp.bfloat16
         halves = range(2)
 
@@ -344,7 +367,7 @@
     def update(it, lo, hi):
         for rr in range(lo, hi, 2 * STEP):
             rows = slice(rr, rr + 2 * STEP)
-            scale = w_own[it][1, rows, :]
+            scale = w_own[it][LANES + rr : LANES + rr + 2 * STEP, :]
             for ch in range(2):
                 grad = own[it][1, ch, rows, :] + (from_left[it][ch, rows, :] + from_right[it][ch, rows, :])
                 value = field[it][1, ch, LANES + rr : LANES + rr + 2 * STEP, :] + grad * scale
@@ -358,14 +381,11 @@
 
     def finish_probe():
         for i in range(N // 8):
-            at = slice(i * 8, i * 8 + 8)
             c, xy = i // (nx * ny), i % (nx * ny)
             for j in range(2):
-                cols = slice(j * LANES, (j + 1) * LANES)
-                scale = 1.0 / (vfull[0][i, j] + PROBE_DAMPING)
                 for q in range(4):
-                    grad = full[0][c, xy // ny, xy % ny, 2 * q + j]
-                    prb[1][q, at, cols] = prb[0][q, at, cols] + grad * scale
+                    value = full[0][c, xy // ny, xy % ny, 2 * q + j]
+                    prb[1][q, i * 8 : i * 8 + 8, j * LANES : (j + 1) * LANES] = value
 
     written = []
 
@@ -385,6 +405,15 @@
     for load in loads:
         load.wait()
     lax.fori_loop(0, SLOTS, order_amplitudes, 0)
+    arrive(tell)
+    facts_in = [
+        pltpu.make_async_copy(src, known.at[t], load_sem.at[len(moves) + 6 + t])
+        for t, src in enumerate((heard.at[0], told, heard.at[1]))
+    ]
+    for copy in facts_in:
+        copy.start()
+    for copy in facts_in:
+        copy.wait()
     rows_w = illuminate(0)
     waiting = spread(field[0], sent_up, sent_down, sent_middle, forwards)
     arrive(waiting)
@@ -402,15 +431,12 @@
         v_x = [remote(vhs[it].at[pl.ds(xs[k] * ny, ny)], vrx[it].at[k - 1], on_x[k]) for k in range(1, nx)]
         v_y = [remote(vhx[it].at[ys[k]], vry[it].at[k - 1], on_y[k]) for k in range(1, ny)]
         v_z = [remote(vz[it].at[z], vz[it].at[z], on_z[k]) for k in range(1, nz)]
-        v_back_y = [remote(mine, mine, on_y[k]) for k in range(1, ny)]
-        row = vfull[it].at[pl.ds((core * nx + x) * ny, ny)]
-        v_back_x = [remote(row, row, on_x[k]) for k in range(1, nx)]
-        whole = vfull[it].at[pl.ds(core * half, half)]
-        v_back_core = remote(whole, whole, partner)
-        w_sides = [
-            remote(w_own[it].at[0], w_right[it], left),
-            remote(w_own[it].at[2], w_left[it], right),
-        ]
+        if it == 1:
+            v_back_y = [remote(mine, mine, on_y[k]) for k in range(1, ny)]
+            row = vfull[it].at[pl.ds((core * nx + x) * ny, ny)]
+            v_back_x = [remote(row, row, on_x[k]) for k in range(1, nx)]
+            whole = vfull[it].at[pl.ds(core * half, half)]
+            v_back_core = remote(whole, whole, partner)
         v_core.start()
 
         def weight_core(it=it, v_core=v_core, v_x=v_x):
@@ -426,13 +452,6 @@
             vhx[it][...] = value
             start(v_y)
 
-        def light_sides(it=it, rows_w=rows_w, w_sides=w_sides):
-            arrive(rows_w)
-            for t in range(3):
-                w_own[it][t, 0:LANES, :] += w_from_up[it][t]
-                w_own[it][t, BAND - LANES : BAND, :] += w_from_dn[it][t]
-            start(w_sides)
-
         def weight_y(it=it, v_y=v_y, v_z=v_z):
             arrive(v_y)
             value = vhx[it][y]
@@ -441,8 +460,8 @@
             vz[it][z] = value
             start(v_z)
 
-        def visit(p, _, it=it, hooks=(weight_core, weight_x, light_sides, weight_y)):
-            for n, hook in zip((1, 2, 2, 3), hooks, strict=True):
+        def visit(p, _, it=it, hooks=(weight_core, weight_x, weight_y)):
+            for n, hook in zip((1, 2, 3), hooks, strict=True):
                 pl.when(p == n)(hook)
             position(it, p)
             return 0
@@ -523,11 +542,13 @@
         for k in range(1, nz):
             value += vz[it][k]
         vfull[it][(core * nx + x) * ny + y] = value
-        start(v_back_y)
-
-        arrive(w_sides)
-        lit = w_own[it][1] + (w_left[it][...] + w_right[it][...])
-        w_own[it][1] = 1.0 / (lit + SAMPLE_DAMPING)
+        if it == 1:
+            start(v_back_y)
+
+        arrive(rows_w)
+        w_own[it][LANES : 2 * LANES, :] += w_from_up[it][...]
+        w_own[it][BAND : LANES + BAND, :] += w_from_dn[it][...]
+        w_own[it][LANES : LANES + BAND, :] = 1.0 / (w_own[it][LANES : LANES + BAND, :] + SAMPLE_DAMPING)
 
         for h, p in enumerate(planes):
             arrive(to_x[h])
@@ -537,8 +558,9 @@
             zb[it][p] = value
         to_z = [send(zb[it].at[zs[k]], rz[it].at[k - 1], on_z[k]) for k in range(1, nz)]
 
-        arrive(v_back_y)
-        start(v_back_x)
+        if it == 1:
+            arrive(v_back_y)
+            start(v_back_x)
 
         arrive(side_middle)
         update(it, *MIDDLE)
@@ -547,6 +569,12 @@
         value = zb[it][z]
         for k in range(nz - 1):
             value += rz[it][k]
+        if it == 0:
+            at = (core * nx + x) * ny + y
+            rows = pl.ds(pl.multiple_of(at * 8, 8), 8)
+            even = lax.broadcasted_iota(jnp.int32, (8, LANES), 0) * 0 + z % 2 == 0
+            base = jnp.where(even, prb[0][z // 2, rows, 0:LANES], prb[0][z // 2, rows, LANES:N])
+            value = base + value / (vfull[0][at, z % 2] + PROBE_DAMPING)
         zg[it][z] = value
         back_z = [send(zg[it].at[z], zg[it].at[z], on_z[k]) for k in range(1, nz)]
 
@@ -565,9 +593,9 @@
         result[core, x, y] = zg[it][...]
         mine = [result.at[core, x, y, p] for p in planes]
         back_x = [[send(m, m, on_x[k]) for k in range(1, nx)] for m in mine]
-        arrive(v_back_x)
-        v_back_core.start()
         if it == 1:
+            arrive(v_back_x)
+            v_back_core.start()
             flush()
 
         arrive(side_down)
@@ -598,13 +626,13 @@
         for h in range(2):
             arrive(back_far[h])
         back_core.append(to_core(2))
-        v_back_core.wait_recv()
         if it == 0:
             arrive(waiting)
             gather(1)
             arrive(back_core)
             finish_probe()
         else:
+            v_back_core.wait_recv()
             write(vfull[1], out_weight)
             flush()
             arrive(back_core)
@@ -675,13 +703,12 @@
                 *two(3, 2, LANES, LANES),
                 *two(2, BAND, LANES),
                 *two(2, BAND, LANES),
-                *two(3, LANES, LANES),
-                *two(3, LANES, LANES),
-                *two(3, BAND, LANES),
-                *two(3, LANES, LANES),
-                *two(3, LANES, LANES),
-                *two(BAND, LANES),
-                *two(BAND, LANES),
+                vmem(8, LANES, dtype=jnp.int32),
+                vmem(2, 8, LANES, dtype=jnp.int32),
+                pltpu.SMEM((3, 8, LANES), jnp.int32),
+                *two(EXT, LANES),
+                *two(LANES, LANES),
+                *two(LANES, LANES),
                 *two(2, nx, ny, 8, 8, LANES),
                 *two(nx, ny, 8, 8, LANES),
                 *two(nx, ny, 8, 8, LANES),
@@ -701,7 +728,7 @@
                 *two(ny - 1, 2, 8, LANES),
                 *two(nz, 2, 8, LANES),
                 *two(blocks, 2, 8, LANES),
-                pltpu.SemaphoreType.DMA((10,)),
+                pltpu.SemaphoreType.DMA((13,)),
                 pltpu.SemaphoreType.DMA((COPIES,)),
                 pltpu.SemaphoreType.DMA((COPIES,)),
             ],

time: 149 us -> 150 us (level)
  no operation moved by 1% of the time
where the time goes in v6:
time: 150 us; the launch traced here: 149 us
  Pallas kernels  148 us (99%)
    pallas_call x1, Pallas kernels, local(): pl.pallas_call(functools.partial(kernel, (nx, ny, nz)), out_shape=[jax.Sh...  144 us
    pallas_call x1, Pallas kernels, local(): pl.pallas_call(functools.partial(finish, 1.0 / math.sqrt(SLOTS * ng * nd)...  4.01 us

profile of v6, /device:TPU:1, one launch (start us, length us, event | category | flops | bytes accessed | tf_op | source)
XLA Modules:
  0.0 149.4 jit_solution(17951678400495863311)
XLA Ops:
  1.3 144.1 %shard_map.94 = (f32[2,512,128]{2,1,0:T(8,128)}, f32[4,256,256]{2,1,0:T(8,128)}, f32[2,4,4,8,8,128]{5,4,3,2,1,0:T(8,128)}, f32[32,2,8,128]{3,2,1,0:T(8,128)}) custom-call(f32[2,512,128]{2,1,0:T(8,128)} %refs_0_.1, f32[4,256,256]{2,1,0:T(8,128)} %bitcast.3, f32[4,256,256]{2,1,0:T(8,128)} %refs_2_.1, bf16[6,256,256]{2,1,0:T(8,128)(2,1)} %constant.2.clone.refs_3_, ...), custom_call_target="tpu_custom_call" | custom-call | flops 8589934592 | bytes 6291456 | tf_op jit(solution)/shard_map/pallas_call | solution.py:676
  145.4 4.0 %shard_map.95 = (f32[2,512,128]{2,1,0:T(8,128)}, f32[2,2,256,256]{3,2,1,0:T(8,128)}, f32[2,2,256,256]{3,2,1,0:T(8,128)}) custom-call(f32[2,512,128]{2,1,0:T(8,128)} %get-tuple-element.7.sample, f32[4,256,256]{2,1,0:T(8,128)} %get-tuple-element.8.probe, f32[32,8,8,128]{3,2,1,0:T(8,128)} %bitcast.2, f32[32,2,8,128]{3,2,1,0:T(8,128)} %get-tuple-element.10.weight), custom_call_target="tpu_custom_call" | custom-call | flops 1048576 | bytes 6291456 | tf_op jit(solution)/shard_map/pallas_call | solution.py:746

commit v7 on v6

--- a/solution.py
+++ b/solution.py
@@ -404,7 +404,6 @@
 
     for load in loads:
         load.wait()
-    lax.fori_loop(0, SLOTS, order_amplitudes, 0)
     arrive(tell)
     facts_in = [
         pltpu.make_async_copy(src, known.at[t], load_sem.at[len(moves) + 6 + t])
@@ -415,8 +414,13 @@
     for copy in facts_in:
         copy.wait()
     rows_w = illuminate(0)
-    waiting = spread(field[0], sent_up, sent_down, sent_middle, forwards)
-    arrive(waiting)
+    arrive(sent_up)
+    forwards += [forward_up(field[0], 0), forward_up(field[0], 2)]
+    lax.fori_loop(0, SLOTS // 2, order_amplitudes, 0)
+    arrive(sent_down)
+    forwards += [forward_down(field[0], 0), forward_down(field[0], 2)]
+    lax.fori_loop(SLOTS // 2, SLOTS, order_amplitudes, 0)
+    arrive(sent_middle + forwards)
 
     half = nx * ny
     for it in range(2):
@@ -516,26 +520,31 @@
             )
         sum_core(3)
 
-        total(grads, own[it], LANES, *UP)
-        total(grads, own[it], LANES, *DOWN)
-
         def add_rows(src, lo, it=it):
             for t in range(3):
                 for ch in range(2):
                     own[it][t, ch, lo : lo + LANES, :] += src[t, ch]
 
-        rows_down.wait_recv()
-        add_rows(from_up[it], UP[0])
-        side_up = send_sides(*UP)
-        rows_up.wait_recv()
-        add_rows(from_dn[it], DOWN[0])
-        side_down = send_sides(*DOWN)
-
+        def edges(it=it, rows_down=rows_down, rows_up=rows_up, send_sides=send_sides, add_rows=add_rows):
+            total(grads, own[it], LANES, *UP)
+            total(grads, own[it], LANES, *DOWN)
+            rows_down.wait_recv()
+            add_rows(from_up[it], UP[0])
+            upper = send_sides(*UP)
+            rows_up.wait_recv()
+            add_rows(from_dn[it], DOWN[0])
+            return upper, send_sides(*DOWN)
+
+        if it == 0:
+            side_up, side_down = edges()
         to_x = []
         for h, p in enumerate(planes):
             arrive(near[h])
             hy[it][h] = hs[it][:, y, p] + (r2[it][0, h] + r2[it][1, h])
             to_x.append([send(hy[it].at[h, xs[k]], rx[it].at[h, k - 1], on_x[k]) for k in range(1, nx)])
+
+        if it == 1:
+            side_up, side_down = edges()
 
         arrive(v_z)
         value = vz[it][0]
@@ -562,8 +571,9 @@
             arrive(v_back_y)
             start(v_back_x)
 
-        arrive(side_middle)
-        update(it, *MIDDLE)
+        if it == 0:
+            arrive(side_middle)
+            update(it, *MIDDLE)
 
         arrive(to_z)
         value = zb[it][z]
@@ -578,9 +588,9 @@
         zg[it][z] = value
         back_z = [send(zg[it].at[z], zg[it].at[z], on_z[k]) for k in range(1, nz)]
 
-        arrive(side_up)
-        update(it, *UP)
         if it == 0:
+            arrive(side_up)
+            update(it, *UP)
 
             def updated(lo, hi):
                 return field[1].at[1, :, LANES + lo : LANES + hi, :]
@@ -598,9 +608,9 @@
             v_back_core.start()
             flush()
 
-        arrive(side_down)
-        update(it, *DOWN)
         if it == 0:
+            arrive(side_down)
+            update(it, *DOWN)
             sent_down = send_columns(field[1], updated, *DOWN)
             forwards.append(forward_down(field[1], 1))
             sent_middle = send_columns(field[1], updated, *MIDDLE)
@@ -632,6 +642,9 @@
             arrive(back_core)
             finish_probe()
         else:
+            for side, rows in ((side_middle, MIDDLE), (side_up, UP), (side_down, DOWN)):
+                arrive(side)
+                update(it, *rows)
             v_back_core.wait_recv()
             write(vfull[1], out_weight)
             flush()

time: 150 us -> 152 us (1.013)
  Pallas kernels: 148 us -> 150 us
    pallas_call x1, Pallas kernels: 144 us -> 146 us  [local(): pl.pallas_call(functools.partial(kernel, (nx, ny, nz)), out_shape=[jax.Sh...]
where the time goes in v7:
time: 152 us
  Pallas kernels  150 us (99%)
    pallas_call x1, Pallas kernels, local(): pl.pallas_call(functools.partial(kernel, (nx, ny, nz)), out_shape=[jax.Sh...  146 us
    pallas_call x1, Pallas kernels, local(): pl.pallas_call(functools.partial(finish, 1.0 / math.sqrt(SLOTS * ng * nd)...  4.01 us

profile of v7, /device:TPU:1, one launch (start us, length us, event | category | flops | bytes accessed | tf_op | source)
XLA Modules:
  0.0 151.6 jit_solution(14655207204074486719)
XLA Ops:
  1.3 146.3 %shard_map.94 = (f32[2,512,128]{2,1,0:T(8,128)}, f32[4,256,256]{2,1,0:T(8,128)}, f32[2,4,4,8,8,128]{5,4,3,2,1,0:T(8,128)}, f32[32,2,8,128]{3,2,1,0:T(8,128)}) custom-call(f32[2,512,128]{2,1,0:T(8,128)} %refs_0_.1, f32[4,256,256]{2,1,0:T(8,128)} %bitcast.3, f32[4,256,256]{2,1,0:T(8,128)} %refs_2_.1, bf16[6,256,256]{2,1,0:T(8,128)(2,1)} %constant.2.clone.refs_3_, ...), custom_call_target="tpu_custom_call" | custom-call | flops 8589934592 | bytes 6291456 | tf_op jit(solution)/shard_map/pallas_call | solution.py:689
  147.6 4.0 %shard_map.95 = (f32[2,512,128]{2,1,0:T(8,128)}, f32[2,2,256,256]{3,2,1,0:T(8,128)}, f32[2,2,256,256]{3,2,1,0:T(8,128)}) custom-call(f32[2,512,128]{2,1,0:T(8,128)} %get-tuple-element.7.sample, f32[4,256,256]{2,1,0:T(8,128)} %get-tuple-element.8.probe, f32[32,8,8,128]{3,2,1,0:T(8,128)} %bitcast.2, f32[32,2,8,128]{3,2,1,0:T(8,128)} %get-tuple-element.10.weight), custom_call_target="tpu_custom_call" | custom-call | flops 1048576 | bytes 6291456 | tf_op jit(solution)/shard_map/pallas_call | solution.py:759

commit v8 on v6

--- a/solution.py
+++ b/solution.py
@@ -470,18 +470,12 @@
 
         sums, mates = part[it], rc[it]
         order = (2, 1, 3, 0)
-        swap = [send(sums.at[1 - core, :, ys[k]], mates.at[:, ys[k]], partner) for k in order]
         planes = [slice(4 * h, 4 * h + 4) for h in range(2)]
 
         total(grads, halo_up[it], 0, 0, LANES)
         rows_up = send(halo_up[it], from_dn[it], above)
         total(grads, halo_dn[it], LANES + BAND, 0, LANES)
         rows_down = send(halo_dn[it], from_up[it], below)
-
-        def sum_core(n, it=it, swap=swap):
-            swap[n].wait_recv()
-            at = ys[order[n]]
-            hs[it][:, at] = part[it][core, :, at] + rc[it][:, at]
 
         def send_sides(lo, hi, it=it):
             return [
@@ -491,6 +485,14 @@
 
         total(grads, own[it], LANES, *MIDDLE)
         side_middle = send_sides(*MIDDLE)
+        swap = [send(sums.at[1 - core, :, ys[k]], mates.at[:, ys[k]], partner) for k in order]
+        total(grads, own[it], LANES, *UP)
+        total(grads, own[it], LANES, *DOWN)
+
+        def sum_core(n, it=it, swap=swap):
+            swap[n].wait_recv()
+            at = ys[order[n]]
+            hs[it][:, at] = part[it][core, :, at] + rc[it][:, at]
 
         sum_core(0)
         far = [
@@ -503,6 +505,18 @@
 
         sum_core(1)
         sum_core(2)
+        def add_rows(src, lo, it=it):
+            for t in range(3):
+                for ch in range(2):
+                    own[it][t, ch, lo : lo + LANES, :] += src[t, ch]
+
+        rows_down.wait_recv()
+        add_rows(from_up[it], UP[0])
+        side_up = send_sides(*UP)
+        rows_up.wait_recv()
+        add_rows(from_dn[it], DOWN[0])
+        side_down = send_sides(*DOWN)
+
         near = []
         for h, p in enumerate(planes):
             arrive(far[h])
@@ -515,21 +529,6 @@
                 ]
             )
         sum_core(3)
-
-        total(grads, own[it], LANES, *UP)
-        total(grads, own[it], LANES, *DOWN)
-
-        def add_rows(src, lo, it=it):
-            for t in range(3):
-                for ch in range(2):
-                    own[it][t, ch, lo : lo + LANES, :] += src[t, ch]
-
-        rows_down.wait_recv()
-        add_rows(from_up[it], UP[0])
-        side_up = send_sides(*UP)
-        rows_up.wait_recv()
-        add_rows(from_dn[it], DOWN[0])
-        side_down = send_sides(*DOWN)
 
         to_x = []
         for h, p in enumerate(planes):

time: 150 us -> 148 us (0.987)
  Pallas kernels: 148 us -> 146 us
    pallas_call x1, Pallas kernels: 144 us -> 142 us  [local(): pl.pallas_call(functools.partial(kernel, (nx, ny, nz)), out_shape=[jax.Sh...]
where the time goes in v8:
time: 148 us; the launch traced here: 147 us
  Pallas kernels  146 us (99%)
    pallas_call x1, Pallas kernels, local(): pl.pallas_call(functools.partial(kernel, (nx, ny, nz)), out_shape=[jax.Sh...  142 us
    pallas_call x1, Pallas kernels, local(): pl.pallas_call(functools.partial(finish, 1.0 / math.sqrt(SLOTS * ng * nd)...  4.01 us

profile of v8, /device:TPU:1, one launch (start us, length us, event | category | flops | bytes accessed | tf_op | source)
XLA Modules:
  0.0 147.4 jit_solution(11596154271096041534)
XLA Ops:
  1.3 142.1 %shard_map.94 = (f32[2,512,128]{2,1,0:T(8,128)}, f32[4,256,256]{2,1,0:T(8,128)}, f32[2,4,4,8,8,128]{5,4,3,2,1,0:T(8,128)}, f32[32,2,8,128]{3,2,1,0:T(8,128)}) custom-call(f32[2,512,128]{2,1,0:T(8,128)} %refs_0_.1, f32[4,256,256]{2,1,0:T(8,128)} %bitcast.3, f32[4,256,256]{2,1,0:T(8,128)} %refs_2_.1, bf16[6,256,256]{2,1,0:T(8,128)(2,1)} %constant.2.clone.refs_3_, ...), custom_call_target="tpu_custom_call" | custom-call | flops 8589934592 | bytes 6291456 | tf_op jit(solution)/shard_map/pallas_call | solution.py:675
  143.4 4.0 %shard_map.95 = (f32[2,512,128]{2,1,0:T(8,128)}, f32[2,2,256,256]{3,2,1,0:T(8,128)}, f32[2,2,256,256]{3,2,1,0:T(8,128)}) custom-call(f32[2,512,128]{2,1,0:T(8,128)} %get-tuple-element.7.sample, f32[4,256,256]{2,1,0:T(8,128)} %get-tuple-element.8.probe, f32[32,8,8,128]{3,2,1,0:T(8,128)} %bitcast.2, f32[32,2,8,128]{3,2,1,0:T(8,128)} %get-tuple-element.10.weight), custom_call_target="tpu_custom_call" | custom-call | flops 1048576 | bytes 6291456 | tf_op jit(solution)/shard_map/pallas_call | solution.py:745
